TPU v7x, 128 devices: a whole 4x4x4 slice. The times are simulated.
128 devices in a mesh: dp: 32 (over y, x, core), mp: 4 (over z).
Axes of the slice: x: 4, y: 4, z: 4, core: 2. Of those that a mesh axis runs over, the one named last changes fastest.
Arguments:
- grads: float32 [32, 2048, 2560], P('dp', None, 'mp'), may hold values from -125 to 125
- errors: float32 [32, 2048, 2560], P('dp', None, 'mp'), may hold values from -6 to 6
- q_init: float32 [2560, 64], P('mp'), may hold values from -6 to 6
- master: float32 [2048, 2560], P('dp', 'mp'), may hold values from -4 to 4
- m_state: float32 [2048, 2560], P('dp', 'mp'), may hold values from -4 to 4
- v_state: float32 [2048, 2560], P('dp', 'mp'), may hold values from 0.01 to 1
Outputs:
- error_new: float32 [32, 2048, 2560], P('dp', None, 'mp')
- q_new: float32 [2560, 64], P('mp')
- master_new: float32 [2048, 2560], P('dp', 'mp')
- m_new: float32 [2048, 2560], P('dp', 'mp')
- v_new: float32 [2048, 2560], P('dp', 'mp')
- weights: bfloat16 [2048, 2560], P(None, 'mp')
All inputs are finite; a program needn't handle non-finite values.
Results may differ from a plain program's by a relative error of at most 0.013.
Values may be sent and summed in bfloat16 or wider, within the bound.
No kernel may reach another device: no remote copies, remote signals or barrier semaphores. Data moves between devices by JAX's collectives and lax.ppermute only.
A program may use at most 64 MiB of HBM per device.

v0:
```python
import jax
import jax.numpy as jnp
from jax import lax
from jax.sharding import PartitionSpec as P

D = 2048
HID = 2560
STEP = 100


beta_first = 0.9
beta_second = 0.95
learning_rate = 0.01
decay_weight = 0.1
adam_eps = 1e-08
norm_eps = 1e-06


def orthonormalise(factor, gram_matrix):
    width = gram_matrix.shape[0]
    jitter = 1e-06 * jnp.trace(gram_matrix) / width + 1e-06
    lower_factor = jnp.linalg.cholesky(gram_matrix + jitter * jnp.eye(width, dtype=jnp.float32))
    return jax.scipy.linalg.solve_triangular(lower_factor, factor.T, lower=True).T


def shards(grads, errors, q_init, master, m_state, v_state):
    highest = lax.Precision.HIGHEST
    merged = grads[0] + errors[0]
    p_sum = lax.psum(jnp.dot(merged, q_init, precision=highest), ("dp", "mp"))
    gram_matrix = jnp.dot(p_sum.T, p_sum, precision=highest)
    p_orth = orthonormalise(p_sum, gram_matrix)
    q_new = lax.psum(
        jnp.dot(merged.T, p_orth, precision=highest).astype(jnp.bfloat16), "dp"
    ).astype(jnp.float32) / lax.axis_size("dp")
    decoded = jnp.dot(p_orth, q_new.T, precision=highest)
    error_new = (merged - decoded)[None]
    shard_rows = master.shape[0]
    owned = lax.dynamic_slice_in_dim(decoded, lax.axis_index("dp") * shard_rows, shard_rows, 0)
    square_total = lax.psum(jnp.sum(owned * owned), ("dp", "mp"))
    update = owned / jnp.sqrt(square_total / (D * HID) + norm_eps)
    m_new = beta_first * m_state + (1.0 - beta_first) * update
    v_new = beta_second * v_state + (1.0 - beta_second) * update * update
    m_hat = m_new / (1.0 - beta_first**STEP)
    v_hat = v_new / (1.0 - beta_second**STEP)
    master_new = master * (1.0 - learning_rate * decay_weight) - learning_rate * m_hat / (
        jnp.sqrt(v_hat) + adam_eps
    )
    weights = lax.all_gather(master_new.astype(jnp.bfloat16), "dp", axis=0, tiled=True)
    return (error_new, q_new, master_new, m_new, v_new, weights)


def solution(mesh):
    in_specs = (
        P("dp", None, "mp"),
        P("dp", None, "mp"),
        P("mp", None),
        P("dp", "mp"),
        P("dp", "mp"),
        P("dp", "mp"),
    )
    out_specs = (
        P("dp", None, "mp"),
        P("mp", None),
        P("dp", "mp"),
        P("dp", "mp"),
        P("dp", "mp"),
        P(None, "mp"),
    )
    return jax.shard_map(shards, mesh=mesh, in_specs=in_specs, out_specs=out_specs, check_vma=False)
```

profile of v0, /device:TPU:1, one launch (start us, length us, event | category | flops | bytes accessed | tf_op | source)
XLA Modules:
  0.0 415.4 jit_solution(14774734529495752173)
XLA Ops:
  7.2 0.0 copy-start
  7.2 0.0 all-reduce.3.cloned.1.call-start
  7.2 0.9 copy-done
  8.1 10.1 %fusion.2 = f32[2048,64]{0,1:T(8,128)} fusion(f32[640,64]{0,1:T(8,128)S(1)} %copy-done, f32[1,2048,640]{2,1,0:T(8,128)} %param.6, f32[1,2048,640]{2,1,0:T(8,128)} %param.7), kind=kOutput, calls=%fused_computation.3 | convolution fusion | flops 1007943680 | bytes 11173888 | tf_op jit(solution)/shard_map/dot_general | solution.py:29
  18.2 0.0 all-reduce.3.cloned.1.call-update
  18.2 0.0 all-reduce.5.cloned.1.call-start
  18.3 148.6 %all-reduce.3.cloned.1.call-done = f32[2048,64]{0,1:T(8,128)} async-done(((f32[2048,64]{0,1:T(8,128)}), f32[2048,64]{0,1:T(8,128)}) %all-reduce.3.cloned.1.call-update) | async-done | bytes 524304 | tf_op jit(solution)/shard_map/psum | solution.py:29
  166.9 2.4 select_reduce_fusion.1
  169.3 0.1 copy.12
  170.0 5.8 %cholesky.17 = f32[64,64]{1,0:T(8,128)S(1)} custom-call(f32[64,64]{1,0:T(8,128)S(1)} %fusion.13), custom_call_target="Cholesky" | custom-call | tf_op jit(solution)/shard_map/jit(cholesky)/cholesky | solution.py:22
  175.9 0.6 compare_reduce_fusion
  176.6 0.7 fusion.9
  177.2 4.9 %custom-call.7 = f32[1,64,64]{1,2,0:T(8,128)S(1)} custom-call(f32[1,64,64]{2,1,0:T(8,128)S(1)} %fusion.9), custom_call_target="InvertDiagBlocksLowerTriangular" | custom-call | tf_op jit(solution)/shard_map/jit(_solve_triangular)/triangular_solve | solution.py:23
  182.1 1.7 fusion.10
  183.8 8.0 %fusion.5 = bf16[640,64]{0,1:T(8,128)(2,1)} fusion(f32[64,2048]{1,0:T(8,128)S(1)} %fusion.10, f32[1,2048,640]{2,1,0:T(8,128)} %param.6, f32[1,2048,640]{2,1,0:T(8,128)} %param.7), kind=kOutput, calls=%fused_computation.6 | convolution fusion | flops 1007984640 | bytes 11091968 | tf_op jit(solution)/shard_map/dot_general | solution.py:33
  191.8 0.0 copy-start.3
  191.8 0.0 copy-start.4
  191.8 0.0 copy-start.5
  191.8 0.0 all-reduce.5.cloned.1.call-update
  191.9 0.2 all-gather.2.cloned.1.call-start
  192.1 95.6 %all-reduce.5.cloned.1.call-done = bf16[640,64]{0,1:T(8,128)(2,1)} async-done(((bf16[640,64]{0,1:T(8,128)(2,1)}), bf16[640,64]{0,1:T(8,128)(2,1)}) %all-reduce.5.cloned.1.call-update) | async-done | bytes 81936 | tf_op jit(solution)/shard_map/psum | solution.py:32
  287.7 0.9 convert_multiply_fusion
  288.6 0.0 copy-start.2
  288.6 4.6 %fusion.18 = f32[2048,640]{1,0:T(8,128)S(1)} fusion(f32[64,2048]{1,0:T(8,128)S(1)} %fusion.10, f32[640,64]{0,1:T(8,128)S(1)} %convert_multiply_fusion), kind=kOutput, calls=%fused_computation.30 | convolution fusion | flops 1006632960 | bytes 5931008 | tf_op jit(solution)/shard_map/dot_general | solution.py:35
  293.2 0.0 copy-start.1
  293.2 2.3 copy-done.1
  295.6 0.6 multiply_reduce_fusion
  296.2 64.5 %psum.23 = f32[]{:T(128)} all-reduce(f32[]{:T(128)} %multiply_reduce_fusion), channel_id=1, replica_groups=mesh['dp'=32,'mp'=4] {'dp','mp'}, use_global_device_ids=true, to_apply=%region_6.7 | all-reduce | flops 1 | bytes 8 | tf_op jit(solution)/shard_map/psum | solution.py:39
  361.4 0.0 copy-done.3
  361.4 0.0 copy-done.4
  361.4 0.0 copy-done.5
  361.4 1.8 fusion.16
  363.2 0.0 all-gather.2.cloned.1.call-update
  363.2 8.7 %fusion.4 = f32[1,2048,640]{2,1,0:T(8,128)} fusion(f32[2048,640]{1,0:T(8,128)} %copy-done.1, f32[1,2048,640]{2,1,0:T(8,128)} %param.6, f32[1,2048,640]{2,1,0:T(8,128)} %param.7), kind=kLoop, calls=%fused_computation.5 | loop fusion | flops 2621440 | bytes 20971520 | tf_op jit(solution)/shard_map/broadcast_in_dim | solution.py:36
  371.9 0.0 copy-done.2
  371.9 33.6 %all-gather.2.cloned.1.call-done = bf16[2048,640]{1,0:T(8,128)(2,1)} async-done(((bf16[64,640]{1,0:T(8,128)(2,1)}), bf16[2048,640]{1,0:T(8,128)(2,1)}) %all-gather.2.cloned.1.call-update) | async-done | bytes 2621456 | tf_op jit(solution)/shard_map/all_gather | solution.py:48
  405.5 3.5 copy.16
  (2 shorter events, 0.0 us)
Async XLA Ops:
  7.2 0.9 copy-start
  7.2 159.7 %all-reduce.3.cloned.1.call-start = ((), (), s32[]{:S(2)}) async-start(), calls=%async_computation | async-start | bytes 1048576 | tf_op jit(solution)/shard_map/psum | solution.py:29
  18.2 269.4 %all-reduce.5.cloned.1.call-start = ((), (), s32[]{:S(2)}) async-start(), calls=%async_computation.1 | async-start | bytes 163840 | tf_op jit(solution)/shard_map/psum | solution.py:32
  191.8 169.6 %copy-start.3 = (f32[64,640]{1,0:T(8,128)S(1)}, f32[64,640]{1,0:T(8,128)}, u32[]{:S(2)}) copy-start(f32[64,640]{1,0:T(8,128)} %param.9) | copy-start | bytes 491524
  191.8 169.6 %copy-start.4 = (f32[64,640]{1,0:T(8,128)S(1)}, f32[64,640]{1,0:T(8,128)}, u32[]{:S(2)}) copy-start(f32[64,640]{1,0:T(8,128)} %param.10) | copy-start | bytes 491524
  191.8 169.6 %copy-start.5 = (f32[64,640]{1,0:T(8,128)S(1)}, f32[64,640]{1,0:T(8,128)}, u32[]{:S(2)}) copy-start(f32[64,640]{1,0:T(8,128)} %param.11) | copy-start | bytes 491524
  191.9 213.6 %all-gather.2.cloned.1.call-start = ((), (), s32[]{:S(2)}) async-start(), calls=%async_computation.2 | async-start | bytes 2703360 | tf_op jit(solution)/shard_map/all_gather | solution.py:48
  288.6 83.3 %copy-start.2 = (f32[640,64]{0,1:T(8,128)}, f32[640,64]{0,1:T(8,128)S(1)}, u32[]{:S(2)}) copy-start(f32[640,64]{0,1:T(8,128)S(1)} %convert_multiply_fusion) | copy-start | bytes 491524
  293.2 2.4 copy-start.1
Sparse Core Ops, SparseCore 0:
  18.4 148.4 all-reduce.2
  192.0 95.6 all-reduce.4
  363.4 42.0 all-gather.1
where the time goes:
time: 416 us; the launch traced here: 415 us
  waiting for transfers between devices  278 us (67%)
  blocking collectives  64.5 us (16%)
  matrix products  26.8 us (6%)
  other arithmetic  24.1 us (6%)
  between operations  15.2 us (4%)
  local copies, waits for them, and re-layouts  6.77 us (2%)
    psum x1, waiting for transfers between devices, shards(): p_sum = lax.psum(jnp.dot(merged, q_init, precision=highest), ('dp', 'mp'))  149 us
    psum x1, waiting for transfers between devices, shards(): lax.psum(jnp.dot(merged.T, p_orth, precision=highest).astype(jnp.bfloat16...  95.6 us
    psum x1, blocking collectives, shards(): square_total = lax.psum(jnp.sum(owned * owned), ('dp', 'mp'))  64.5 us
    all_gather x1, waiting for transfers between devices, shards(): lax.all_gather(master_new.astype(jnp.bfloat16), 'dp', axis=0, tiled=True)  33.6 us
    dot_general x1, matrix products, shards(): p_sum = lax.psum(jnp.dot(merged, q_init, precision=highest), ('dp', 'mp'))  10.1 us
    broadcast_in_dim x1, other arithmetic, shards(): error_new = (merged - decoded)[None]  8.66 us
  transfers between devices with their start and end apart: 3, of which 3 were waited for; matrix products, arithmetic and copies ran while one was open for 2% of the time, Pallas kernels for 0%

commit v1 on v0

v1 whole, which is shorter than its diff:
```python
import jax
import jax.numpy as jnp
from jax import lax
from jax.experimental import pallas as pl
from jax.experimental.pallas import tpu as pltpu
from jax.sharding import PartitionSpec as P

D = 2048
HID = 2560
STEP = 100
RANK = 64
REPLICAS = 32
HALF = D // 2
COLS = 640
ROWS = 64

beta_first = 0.9
beta_second = 0.95
learning_rate = 0.01
decay_weight = 0.1
adam_eps = 1e-08
norm_eps = 1e-06

f32 = jnp.float32
bf16 = jnp.bfloat16
HIGHEST = lax.Precision.HIGHEST
VMEM_BYTES = 48 * 1024 * 1024
LEFT_CHUNKS = 8
BLOCK = 256


def split(x):
    high = x.astype(bf16)
    return high, (x - high.astype(f32)).astype(bf16)


def dot(a, b, ca, cb, precision=None):
    return lax.dot_general(
        a, b, (((ca,), (cb,)), ((), ())), precision=precision, preferred_element_type=f32
    )


def lanes(shape):
    return lax.broadcasted_iota(jnp.int32, shape, len(shape) - 1)


def left_kernel(grads, errors, q_ref, merged_ref, part_ref, buffer, sems):
    size = HALF // LEFT_CHUNKS
    copies = []
    for c in range(LEFT_CHUNKS):
        rows = pl.ds(c * size, size)
        pair = (
            pltpu.make_async_copy(grads.at[:, rows], merged_ref.at[:, rows], sems.at[0, c]),
            pltpu.make_async_copy(errors.at[:, rows], buffer.at[:, rows], sems.at[1, c]),
        )
        for copy in pair:
            copy.start()
        copies.append(pair)
    q = q_ref[...]
    q_high = q.astype(bf16).astype(f32)
    right = jnp.concatenate([q_high, q - q_high], axis=1).astype(bf16)
    low_lanes = lanes((size, 2 * RANK)) < RANK
    for c in range(LEFT_CHUNKS):
        for copy in copies[c]:
            copy.wait()
        rows = pl.ds(c * size, size)
        merged = merged_ref[:, rows] + buffer[:, rows]
        merged_ref[:, rows] = merged
        high, low = split(merged.reshape(2 * size, COLS))
        part = dot(high, right, 1, 0) + dot(low, right, 1, 0)
        part = part + pltpu.roll(part, RANK, 1)
        part_ref[rows, :] = jnp.where(low_lanes, part[:size], part[size:]).astype(bf16)


def left(grads, errors, q_init):
    return pl.pallas_call(
        left_kernel,
        out_shape=(
            jax.ShapeDtypeStruct((2, HALF, COLS), f32),
            jax.ShapeDtypeStruct((HALF, 2 * RANK), bf16),
        ),
        in_specs=[
            pl.BlockSpec(memory_space=pl.ANY),
            pl.BlockSpec(memory_space=pl.ANY),
            pl.BlockSpec(memory_space=pltpu.VMEM),
        ],
        out_specs=(
            pl.BlockSpec(memory_space=pltpu.VMEM),
            pl.BlockSpec(memory_space=pltpu.VMEM),
        ),
        scratch_shapes=[
            pltpu.VMEM((2, HALF, COLS), f32),
            pltpu.SemaphoreType.DMA((2, LEFT_CHUNKS)),
        ],
        compiler_params=pltpu.CompilerParams(vmem_limit_bytes=VMEM_BYTES),
        name="left_factor",
    )(grads.reshape(2, HALF, COLS), errors.reshape(2, HALF, COLS), q_init)


def sum_kernel(parts_ref, out_ref):
    total = jnp.sum(parts_ref[...].astype(f32).reshape(out_ref.shape), axis=0, keepdims=True)
    out_ref[...] = jnp.broadcast_to(total, out_ref.shape)


def sum_repeat(parts):
    return pl.pallas_call(
        sum_kernel,
        out_shape=jax.ShapeDtypeStruct((128, 8, 128), f32),
        in_specs=[pl.BlockSpec(memory_space=pltpu.VMEM)],
        out_specs=pl.BlockSpec(memory_space=pltpu.VMEM),
        compiler_params=pltpu.CompilerParams(vmem_limit_bytes=VMEM_BYTES),
        name="sum_repeat",
    )(parts)


def inverse_factor(gram):
    row_id = lax.broadcasted_iota(jnp.int32, (RANK, 2 * RANK), 0)
    lane = lanes((RANK, 2 * RANK))
    eye = jnp.where(row_id == lane, 1.0, 0.0).astype(f32)
    trace = jnp.sum(gram * eye, keepdims=True)
    jitter = 1e-06 * trace / RANK + 1e-06
    start = jnp.where(lane < RANK, gram + jitter * eye, jnp.where(row_id == lane - RANK, 1.0, 0.0))
    tiles = [start[8 * k : 8 * k + 8] for k in range(RANK // 8)]
    sub = lax.broadcasted_iota(jnp.int32, (8, 1), 0)
    for j in range(RANK - 1):
        t, r = divmod(j, 8)
        row = tiles[t][r : r + 1]
        row = row * (1.0 / row[:, j : j + 1])
        for k in range(t, RANK // 8):
            factor = tiles[k][:, j : j + 1]
            if k == t:
                factor = jnp.where(sub > r, factor, 0.0)
            tiles[k] = tiles[k] - factor * row
    done = jnp.concatenate(tiles, axis=0)
    pivots = jnp.sum(done * eye, axis=1, keepdims=True)
    return jnp.where(lane < RANK, 0.0, done * (1.0 / jnp.sqrt(pivots)))


def pair_rows(packed):
    low_lanes = lanes(packed.shape) < RANK
    high = packed.astype(bf16).astype(f32)
    low = packed - high
    top = jnp.where(low_lanes, high, pltpu.roll(low, RANK, 1)).astype(bf16)
    bottom = jnp.where(low_lanes, pltpu.roll(high, RANK, 1), low).astype(bf16)
    return top, bottom


def right_kernel(p_ref, merged_ref, orth_ref, square_ref, part_ref):
    packed = p_ref[...]
    gram = dot(packed, packed, 0, 0, HIGHEST)
    shifted = pltpu.roll(gram[RANK:], RANK, 1)
    gram = gram[:RANK] + shifted
    inverse = inverse_factor(gram)

    pairs = pair_rows(packed)
    acc = jnp.zeros((2 * RANK, COLS), f32)
    for half in range(2):
        for c in range(4):
            rows = slice(c * BLOCK, (c + 1) * BLOCK)
            high, low = split(merged_ref[half, rows])
            acc = acc + (dot(pairs[half][rows], high, 0, 0) + dot(pairs[half][rows], low, 0, 0))
    part = acc[:RANK] + acc[RANK:]

    both = jnp.concatenate([pltpu.roll(inverse, RANK, 1), inverse], axis=0)
    inverse_small = both[:RANK, :RANK]
    part_ref[...] = (dot(inverse_small, part, 1, 0, HIGHEST) * (1.0 / REPLICAS)).astype(bf16)
    orth = dot(packed, both, 1, 1, HIGHEST)
    square = dot(orth, orth, 0, 0, HIGHEST)
    square_ref[...] = square[:RANK] + pltpu.roll(square[RANK:], RANK, 1)
    top, bottom = pair_rows(orth)
    orth_ref[:HALF] = top
    orth_ref[HALF:] = bottom


def right(packed, merged):
    return pl.pallas_call(
        right_kernel,
        out_shape=(
            jax.ShapeDtypeStruct((D, 2 * RANK), bf16),
            jax.ShapeDtypeStruct((RANK, 2 * RANK), f32),
            jax.ShapeDtypeStruct((RANK, COLS), bf16),
        ),
        in_specs=[pl.BlockSpec(memory_space=pltpu.VMEM)] * 2,
        out_specs=(pl.BlockSpec(memory_space=pltpu.VMEM),) * 3,
        compiler_params=pltpu.CompilerParams(vmem_limit_bytes=VMEM_BYTES),
        name="right_factor",
    )(packed, merged)


def adam(update, master, m_state, v_state):
    m_new = beta_first * m_state + (1.0 - beta_first) * update
    v_new = beta_second * v_state + (1.0 - beta_second) * update * update
    m_hat = m_new / (1.0 - beta_first**STEP)
    v_hat = v_new / (1.0 - beta_second**STEP)
    master_new = master * (1.0 - learning_rate * decay_weight) - learning_rate * m_hat / (
        jnp.sqrt(v_hat) + adam_eps
    )
    return m_new, v_new, master_new


def final_kernel(
    q_ref,
    orth_ref,
    square_ref,
    merged_ref,
    states_ref,
    master_ref,
    m_ref,
    v_ref,
    error_ref,
    weights_ref,
    q_out,
    master_out,
    m_out,
    v_out,
    both_ref,
    scale_ref,
):
    step = pl.program_id(0)

    @pl.when(step == 0)
    def _():
        gram = jnp.zeros((RANK, RANK), f32)
        for z in range(4):
            gram = gram + dot(q_ref[z], q_ref[z], 1, 1)
        total = jnp.sum(gram * square_ref[:, :RANK], keepdims=True)
        scale = 1.0 / jnp.sqrt(total / (D * HID) + norm_eps)
        scale_ref[...] = jnp.broadcast_to(scale, scale_ref.shape)
        q = q_ref[lax.axis_index("mp")]
        both_ref[:RANK] = q
        both_ref[RANK:] = q
        q_out[...] = q.astype(f32).T
        start = pl.multiple_of(lax.axis_index("dp") * ROWS, ROWS)
        decoded = dot(orth_ref[pl.ds(start, ROWS)], both_ref[...], 1, 0)
        m_new, v_new, master_new = adam(decoded * scale, master_ref[...], m_ref[...], v_ref[...])
        m_out[...] = m_new
        v_out[...] = v_new
        master_out[...] = master_new

    rows = pl.ds(pl.multiple_of(step * BLOCK, BLOCK), BLOCK)
    decoded = dot(orth_ref[rows], both_ref[...], 1, 0)
    error_ref[...] = merged_ref[...] - decoded
    update = decoded * scale_ref[:1, :1]
    for k in range(BLOCK // ROWS):
        part = slice(k * ROWS, (k + 1) * ROWS)
        state = [states_ref[k, n].astype(f32) for n in range(3)]
        weights_ref[part] = adam(update[part], *state)[2].astype(bf16)


def final(q_all, orth, square, merged, states, master, m_state, v_state):
    steps = D // BLOCK
    whole = lambda *shape: pl.BlockSpec(shape, lambda i: (0,) * len(shape))
    return pl.pallas_call(
        final_kernel,
        grid=(steps,),
        out_shape=(
            jax.ShapeDtypeStruct((D, COLS), f32),
            jax.ShapeDtypeStruct((D, COLS), bf16),
            jax.ShapeDtypeStruct((COLS, RANK), f32),
            jax.ShapeDtypeStruct((ROWS, COLS), f32),
            jax.ShapeDtypeStruct((ROWS, COLS), f32),
            jax.ShapeDtypeStruct((ROWS, COLS), f32),
        ),
        in_specs=[
            whole(4, RANK, COLS),
            whole(D, 2 * RANK),
            whole(RANK, 2 * RANK),
            pl.BlockSpec((BLOCK, COLS), lambda i: (i, 0)),
            pl.BlockSpec((BLOCK // ROWS, 3, ROWS, COLS), lambda i: (i, 0, 0, 0)),
            whole(ROWS, COLS),
            whole(ROWS, COLS),
            whole(ROWS, COLS),
        ],
        out_specs=(
            pl.BlockSpec((BLOCK, COLS), lambda i: (i, 0)),
            pl.BlockSpec((BLOCK, COLS), lambda i: (i, 0)),
            whole(COLS, RANK),
            whole(ROWS, COLS),
            whole(ROWS, COLS),
            whole(ROWS, COLS),
        ),
        scratch_shapes=[pltpu.VMEM((2 * RANK, COLS), bf16), pltpu.VMEM((8, 128), f32)],
        compiler_params=pltpu.CompilerParams(vmem_limit_bytes=VMEM_BYTES),
        name="decode_update",
    )(q_all, orth, square, merged, states, master, m_state, v_state)


def shards(grads, errors, q_init, master, m_state, v_state):
    states = jnp.stack([master, m_state, v_state]).astype(bf16)
    states = lax.all_gather(states, "dp", axis=0, tiled=False)
    merged, part = left(grads, errors, q_init)
    parts = lax.all_to_all(part.reshape(128, 8, 128), ("dp", "mp"), 0, 0)
    owned = sum_repeat(parts.reshape(HALF, 128))
    packed = lax.all_to_all(owned, ("dp", "mp"), 0, 0).reshape(HALF, 128)
    orth, square, q_part = right(packed, merged)
    q_parts = lax.all_to_all(q_part.reshape(32, 2, COLS), "dp", 0, 0)
    q_owned = jnp.sum(q_parts.astype(f32), axis=0).astype(bf16)
    q_owned = jnp.broadcast_to(q_owned[None], (128, 2, COLS))
    q_all = lax.all_to_all(q_owned, ("mp", "dp"), 0, 0).reshape(4, RANK, COLS)
    error_new, weights, q_new, master_new, m_new, v_new = final(
        q_all, orth, square, merged.reshape(D, COLS), states, master, m_state, v_state
    )
    return (error_new[None], q_new, master_new, m_new, v_new, weights)


def solution(mesh):
    in_specs = (
        P("dp", None, "mp"),
        P("dp", None, "mp"),
        P("mp", None),
        P("dp", "mp"),
        P("dp", "mp"),
        P("dp", "mp"),
    )
    out_specs = (
        P("dp", None, "mp"),
        P("mp", None),
        P("dp", "mp"),
        P("dp", "mp"),
        P("dp", "mp"),
        P(None, "mp"),
    )
    return jax.shard_map(shards, mesh=mesh, in_specs=in_specs, out_specs=out_specs, check_vma=False)
```

time: 416 us -> 123 us (0.30)
  waiting for transfers between devices: 278 us -> 0.04 us
  Pallas kernels: 0 us -> 28.8 us
  matrix products: 26.8 us -> 0 us
  other arithmetic: 24.1 us -> 2.77 us
  blocking collectives: 64.5 us -> 72.6 us
    psum x2 -> x0, waiting for transfers between devices: 244 us -> none  [the longest x1 149 us: shards(): p_sum = lax.psum(jnp.dot(merged, q_init, precision=highest), ('dp', 'mp'))]
    all_to_all x0 -> x4, blocking collectives: none -> 72.6 us  [the longest x1 23.3 us: shards(): parts = lax.all_to_all(part.reshape(128, 8, 128), ('dp', 'mp'), 0, 0)]
    psum x1 -> x0, blocking collectives: 64.5 us -> none  [shards(): square_total = lax.psum(jnp.sum(owned * owned), ('dp', 'mp'))]
    all_gather x1, waiting for transfers between devices: 33.6 us -> 0.02 us  [shards(): states = lax.all_gather(states, 'dp', axis=0, tiled=False)]
    pallas_call x0 -> x4, Pallas kernels: none -> 28.8 us  [the longest x1 12.4 us: final(): pl.pallas_call(final_kernel, grid=(steps,), out_shape=(jax.ShapeDtypeStru...]
    dot_general x4 -> x0, matrix products: 25.1 us -> none  [the longest x1 10.1 us: shards(): p_sum = lax.psum(jnp.dot(merged, q_init, precision=highest), ('dp', 'mp'))]
    another operation x5 -> x3, other arithmetic: 12.1 us -> 2.68 us  [shards(): states = jnp.stack([master, m_state, v_state]).astype(bf16)]
    broadcast_in_dim x1 -> x0, other arithmetic: 8.66 us -> none  [shards(): error_new = (merged - decoded)[None]]
  transfers between devices with their start and end apart: 3 -> 1, of which waited for: 3 -> 0; matrix products, arithmetic and copies ran while one was open for 2% -> 1% of each run, Pallas kernels for 0% -> 13%
where the time goes in v1:
time: 123 us
  blocking collectives  72.6 us (59%)
  Pallas kernels  28.8 us (23%)
  between operations  14.1 us (11%)
  local copies, waits for them, and re-layouts  4.57 us (4%)
  other arithmetic  2.77 us (2%)
    all_to_all x1, blocking collectives, shards(): parts = lax.all_to_all(part.reshape(128, 8, 128), ('dp', 'mp'), 0, 0)  23.3 us
    all_to_all x1, blocking collectives, shards(): packed = lax.all_to_all(owned, ('dp', 'mp'), 0, 0).reshape(HALF, 128)  20 us
    all_to_all x1, blocking collectives, shards(): q_all = lax.all_to_all(q_owned, ('mp', 'dp'), 0, 0).reshape(4, RANK, COLS)  15.4 us
    all_to_all x1, blocking collectives, shards(): q_parts = lax.all_to_all(q_part.reshape(32, 2, COLS), 'dp', 0, 0)  14 us
    pallas_call x1, Pallas kernels, final(): pl.pallas_call(final_kernel, grid=(steps,), out_shape=(jax.ShapeDtypeStru...  12.4 us
    pallas_call x1, Pallas kernels, right(): pl.pallas_call(right_kernel, out_shape=(jax.ShapeDtypeStruct((D, 2 * RANK...  11.2 us
    pallas_call x1, Pallas kernels, left(): pl.pallas_call(left_kernel, out_shape=(jax.ShapeDtypeStruct((2, HALF, COL...  4.95 us
    unnamed x10, local copies, waits for them, and re-layouts  4.23 us
  transfers between devices with their start and end apart: 1, of which 0 were waited for; matrix products, arithmetic and copies ran while one was open for 1% of the time, Pallas kernels for 13%

profile of v1, /device:TPU:1, one launch (start us, length us, event | category | flops | bytes accessed | tf_op | source)
XLA Modules:
  0.0 122.9 jit_solution(9084935671204972898)
XLA Ops:
  7.2 0.0 all-gather.2.cloned.1.call-start
  7.2 0.9 convert_bitcast_fusion.2
  8.1 1.0 convert_bitcast_fusion
  9.2 0.7 pad_maximum_fusion
  9.9 0.0 all-gather.2.cloned.1.call-update
  9.9 1.1 copy.14.q_ref
  11.0 4.9 %left_factor.1 = (f32[2,1024,640]{2,1,0:T(8,128)S(1)}, bf16[1024,128]{1,0:T(8,128)(2,1)S(1)}) custom-call(f32[2,1024,640]{2,1,0:T(8,128)} %bitcast.17, f32[2,1024,640]{2,1,0:T(8,128)} %bitcast.18, f32[640,64]{1,0:T(8,128)S(1)} %copy.14.q_ref), custom_call_target="tpu_custom_call" | custom-call | tf_op jit(solution)/shard_map/left_factor/pallas_call | solution.py:76
  16.0 0.0 copy-start
  16.0 2.3 %copy-done = f32[2,1024,640]{2,1,0:T(8,128)} copy-done((f32[2,1024,640]{2,1,0:T(8,128)}, f32[2,1024,640]{2,1,0:T(8,128)S(1)}, u32[]{:S(2)}) %copy-start) | copy-done | bytes 5242904
  18.3 0.0 copy-start.1
  18.3 0.0 copy-start.2
  18.3 0.0 copy-start.3
  18.3 23.3 %all_to_all.20 = bf16[128,8,128]{2,1,0:T(8,128)(2,1)S(1)} all-to-all(bf16[128,8,128]{2,1,0:T(8,128)(2,1)S(1)} %bitcast.16), channel_id=1, replica_groups=mesh['dp'=32,'mp'=4] {'dp','mp'}, dimensions={0} | all-to-all | bytes 524288 | tf_op jit(solution)/shard_map/all_to_all | solution.py:292
  41.6 0.2 sum_repeat.1
  41.7 20.0 %all_to_all.21 = f32[128,8,128]{2,1,0:T(8,128)S(1)} all-to-all(f32[128,8,128]{2,1,0:T(8,128)S(1)} %sum_repeat.1), channel_id=1, replica_groups=mesh['dp'=32,'mp'=4] {'dp','mp'}, dimensions={0} | all-to-all | bytes 1048576 | tf_op jit(solution)/shard_map/all_to_all | solution.py:294
  61.7 11.2 %right_factor.1 = (bf16[2048,128]{1,0:T(8,128)(2,1)S(1)}, f32[64,128]{1,0:T(8,128)S(1)}, bf16[64,640]{1,0:T(8,128)(2,1)S(1)}) custom-call(f32[1024,128]{1,0:T(8,128)S(1)} %bitcast.14, f32[2,1024,640]{2,1,0:T(8,128)} %copy-done), custom_call_target="tpu_custom_call" | custom-call | tf_op jit(solution)/shard_map/right_factor/pallas_call | solution.py:176
  73.0 14.0 %all_to_all.22 = bf16[32,2,640]{2,1,0:T(2,128)(2,1)S(1)} all-to-all(bf16[32,2,640]{2,1,0:T(2,128)(2,1)S(1)} %reshape.90), channel_id=1, replica_groups=mesh['dp'=32,'mp'=4] {'dp'}, dimensions={0} | all-to-all | bytes 163840 | tf_op jit(solution)/shard_map/all_to_all | solution.py:296
  87.0 0.1 reduce_sum.12
  87.1 0.2 broadcast_in_dim.4
  87.2 15.4 %all_to_all.23 = bf16[128,2,640]{2,1,0:T(2,128)(2,1)S(1)} all-to-all(bf16[128,2,640]{2,1,0:T(2,128)(2,1)S(1)} %broadcast_in_dim.4), channel_id=1, replica_groups=mesh['dp'=32,'mp'=4] {'mp','dp'}, dimensions={0} | all-to-all | bytes 655360 | tf_op jit(solution)/shard_map/all_to_all | solution.py:299
  102.7 0.1 reshape.91.q_ref
  102.8 0.0 all-gather.2.cloned.1.call-done.states_ref
  102.8 0.0 copy-done.1
  102.8 0.0 copy-done.2
  102.8 0.0 copy-done.3
  102.8 12.4 %decode_update.1 = (f32[2048,640]{1,0:T(8,128)}, bf16[2048,640]{1,0:T(8,128)(2,1)}, f32[640,64]{1,0:T(8,128)S(1)}, f32[64,640]{1,0:T(8,128)}, f32[64,640]{1,0:T(8,128)}, /*index=5*/f32[64,640]{1,0:T(8,128)}) custom-call(bf16[4,64,640]{2,1,0:T(8,128)(2,1)S(1)} %reshape.91.q_ref, bf16[2048,128]{1,0:T(8,128)(2,1)S(1)} %get-tuple-element.20.orth_ref, ...), custom_call_target="tpu_custom_call" | custom-call | tf_op jit(solution)/shard_map/decode_update/pallas_call | solution.py:253
  115.3 0.8 copy.15
  (1 shorter events, 0.0 us)
Async XLA Ops:
  7.2 95.6 %all-gather.2.cloned.1.call-start = ((), (), s32[]{:S(2)}) async-start(), calls=%async_computation.4 | async-start | bytes 8110080 | tf_op jit(solution)/shard_map/all_gather | solution.py:290
  16.0 2.3 %copy-start = (f32[2,1024,640]{2,1,0:T(8,128)}, f32[2,1024,640]{2,1,0:T(8,128)S(1)}, u32[]{:S(2)}) copy-start(f32[2,1024,640]{2,1,0:T(8,128)S(1)} %get-tuple-element.18.merged_ref) | copy-start | bytes 15728644
  18.3 84.5 %copy-start.1 = (f32[64,640]{1,0:T(8,128)S(1)}, f32[64,640]{1,0:T(8,128)}, u32[]{:S(2)}) copy-start(f32[64,640]{1,0:T(8,128)} %v_ref.1) | copy-start | bytes 491524
  18.3 84.5 %copy-start.2 = (f32[64,640]{1,0:T(8,128)S(1)}, f32[64,640]{1,0:T(8,128)}, u32[]{:S(2)}) copy-start(f32[64,640]{1,0:T(8,128)} %m_ref.1) | copy-start | bytes 491524
  18.3 84.5 %copy-start.3 = (f32[64,640]{1,0:T(8,128)S(1)}, f32[64,640]{1,0:T(8,128)}, u32[]{:S(2)}) copy-start(f32[64,640]{1,0:T(8,128)} %master_ref.1) | copy-start | bytes 491524
Sparse Core Ops, SparseCore 0:
  10.8 62.3 all-gather.1

commit v2 on v1

--- a/solution.py
+++ b/solution.py
@@ -24,7 +24,7 @@
 f32 = jnp.float32
 bf16 = jnp.bfloat16
 HIGHEST = lax.Precision.HIGHEST
-VMEM_BYTES = 48 * 1024 * 1024
+MIB = 1024 * 1024
 LEFT_CHUNKS = 8
 BLOCK = 256
 
@@ -40,12 +40,25 @@
     )
 
 
+def hbm(x):
+    return pltpu.with_memory_space_constraint(x, pltpu.HBM)
+
+
 def lanes(shape):
     return lax.broadcasted_iota(jnp.int32, shape, len(shape) - 1)
 
 
-def left_kernel(grads, errors, q_ref, merged_ref, part_ref, buffer, sems):
+def left_kernel(
+    grads, errors, q_hbm, master, m_state, v_state,
+    merged_ref, part_ref, states_ref,
+    buffer, q_buffer, state_buffer, sems, small_sems,
+):
     size = HALF // LEFT_CHUNKS
+    small = [pltpu.make_async_copy(q_hbm, q_buffer, small_sems.at[0])]
+    for n, source in enumerate((master, m_state, v_state)):
+        small.append(pltpu.make_async_copy(source, state_buffer.at[n], small_sems.at[n + 1]))
+    for copy in small:
+        copy.start()
     copies = []
     for c in range(LEFT_CHUNKS):
         rows = pl.ds(c * size, size)
@@ -56,9 +69,13 @@
         for copy in pair:
             copy.start()
         copies.append(pair)
-    q = q_ref[...]
+    small[0].wait()
+    q = q_buffer[...]
     q_high = q.astype(bf16).astype(f32)
-    right = jnp.concatenate([q_high, q - q_high], axis=1).astype(bf16)
+    right = jnp.concatenate([q_high, q - q_high], axis=0).T.astype(bf16)
+    for n in range(3):
+        small[n + 1].wait()
+        states_ref[n] = state_buffer[n].astype(bf16)
     low_lanes = lanes((size, 2 * RANK)) < RANK
     for c in range(LEFT_CHUNKS):
         for copy in copies[c]:
@@ -72,29 +89,29 @@
         part_ref[rows, :] = jnp.where(low_lanes, part[:size], part[size:]).astype(bf16)
 
 
-def left(grads, errors, q_init):
+def left(grads, errors, q_init, master, m_state, v_state):
     return pl.pallas_call(
         left_kernel,
         out_shape=(
             jax.ShapeDtypeStruct((2, HALF, COLS), f32),
             jax.ShapeDtypeStruct((HALF, 2 * RANK), bf16),
+            jax.ShapeDtypeStruct((3, ROWS, COLS), bf16),
         ),
-        in_specs=[
-            pl.BlockSpec(memory_space=pl.ANY),
-            pl.BlockSpec(memory_space=pl.ANY),
-            pl.BlockSpec(memory_space=pltpu.VMEM),
-        ],
-        out_specs=(
-            pl.BlockSpec(memory_space=pltpu.VMEM),
-            pl.BlockSpec(memory_space=pltpu.VMEM),
-        ),
+        in_specs=[pl.BlockSpec(memory_space=pltpu.HBM)] * 6,
+        out_specs=(pl.BlockSpec(memory_space=pltpu.VMEM),) * 3,
         scratch_shapes=[
             pltpu.VMEM((2, HALF, COLS), f32),
+            pltpu.VMEM((RANK, COLS), f32),
+            pltpu.VMEM((3, ROWS, COLS), f32),
             pltpu.SemaphoreType.DMA((2, LEFT_CHUNKS)),
+            pltpu.SemaphoreType.DMA((4,)),
         ],
-        compiler_params=pltpu.CompilerParams(vmem_limit_bytes=VMEM_BYTES),
+        compiler_params=pltpu.CompilerParams(vmem_limit_bytes=20 * MIB),
         name="left_factor",
-    )(grads.reshape(2, HALF, COLS), errors.reshape(2, HALF, COLS), q_init)
+    )(
+        hbm(grads.reshape(2, HALF, COLS)), hbm(errors.reshape(2, HALF, COLS)), hbm(q_init.T),
+        hbm(master), hbm(m_state), hbm(v_state),
+    )
 
 
 def sum_kernel(parts_ref, out_ref):
@@ -108,7 +125,7 @@
         out_shape=jax.ShapeDtypeStruct((128, 8, 128), f32),
         in_specs=[pl.BlockSpec(memory_space=pltpu.VMEM)],
         out_specs=pl.BlockSpec(memory_space=pltpu.VMEM),
-        compiler_params=pltpu.CompilerParams(vmem_limit_bytes=VMEM_BYTES),
+        compiler_params=pltpu.CompilerParams(vmem_limit_bytes=16 * MIB),
         name="sum_repeat",
     )(parts)
 
@@ -182,7 +199,7 @@
         ),
         in_specs=[pl.BlockSpec(memory_space=pltpu.VMEM)] * 2,
         out_specs=(pl.BlockSpec(memory_space=pltpu.VMEM),) * 3,
-        compiler_params=pltpu.CompilerParams(vmem_limit_bytes=VMEM_BYTES),
+        compiler_params=pltpu.CompilerParams(vmem_limit_bytes=16 * MIB),
         name="right_factor",
     )(packed, merged)
 
@@ -198,97 +215,113 @@
     return m_new, v_new, master_new
 
 
+def new_weights(update, master, m_state, v_state):
+    first = learning_rate / (1.0 - beta_first**STEP)
+    second = 1.0 / (1.0 - beta_second**STEP)
+    top = (first * beta_first) * m_state + (first * (1.0 - beta_first)) * update
+    square = (second * beta_second) * v_state + (second * (1.0 - beta_second)) * (update * update)
+    root = square * lax.rsqrt(square) + adam_eps
+    return (1.0 - learning_rate * decay_weight) * master - top * pl.reciprocal(root, approx=True)
+
+
 def final_kernel(
-    q_ref,
-    orth_ref,
-    square_ref,
-    merged_ref,
-    states_ref,
-    master_ref,
-    m_ref,
-    v_ref,
-    error_ref,
-    weights_ref,
-    q_out,
-    master_out,
-    m_out,
-    v_out,
-    both_ref,
-    scale_ref,
+    q_ref, orth_ref, square_ref, merged_ref, states_hbm, master_ref, m_ref, v_ref,
+    error_hbm, weights_hbm, q_hbm, master_hbm, m_hbm, v_hbm,
+    states_ref, error_ref, weights_ref, q_out, owned_ref, both_ref,
+    in_sems, error_sems, weight_sems, small_sems,
 ):
-    step = pl.program_id(0)
-
-    @pl.when(step == 0)
-    def _():
-        gram = jnp.zeros((RANK, RANK), f32)
-        for z in range(4):
-            gram = gram + dot(q_ref[z], q_ref[z], 1, 1)
-        total = jnp.sum(gram * square_ref[:, :RANK], keepdims=True)
-        scale = 1.0 / jnp.sqrt(total / (D * HID) + norm_eps)
-        scale_ref[...] = jnp.broadcast_to(scale, scale_ref.shape)
-        q = q_ref[lax.axis_index("mp")]
-        both_ref[:RANK] = q
-        both_ref[RANK:] = q
-        q_out[...] = q.astype(f32).T
-        start = pl.multiple_of(lax.axis_index("dp") * ROWS, ROWS)
-        decoded = dot(orth_ref[pl.ds(start, ROWS)], both_ref[...], 1, 0)
-        m_new, v_new, master_new = adam(decoded * scale, master_ref[...], m_ref[...], v_ref[...])
-        m_out[...] = m_new
-        v_out[...] = v_new
-        master_out[...] = master_new
-
-    rows = pl.ds(pl.multiple_of(step * BLOCK, BLOCK), BLOCK)
-    decoded = dot(orth_ref[rows], both_ref[...], 1, 0)
-    error_ref[...] = merged_ref[...] - decoded
-    update = decoded * scale_ref[:1, :1]
-    for k in range(BLOCK // ROWS):
-        part = slice(k * ROWS, (k + 1) * ROWS)
-        state = [states_ref[k, n].astype(f32) for n in range(3)]
-        weights_ref[part] = adam(update[part], *state)[2].astype(bf16)
+    steps = D // BLOCK
+    per = BLOCK // ROWS
+
+    def states_copy(c):
+        part = pl.ds(c * per, per)
+        return pltpu.make_async_copy(states_hbm.at[part], states_ref.at[part], in_sems.at[c])
+
+    def out_copies(c):
+        rows = pl.ds(pl.multiple_of(c * BLOCK, BLOCK), BLOCK)
+        return (
+            pltpu.make_async_copy(error_ref.at[rows], error_hbm.at[rows], error_sems.at[c]),
+            pltpu.make_async_copy(weights_ref.at[rows], weights_hbm.at[rows], weight_sems.at[c]),
+        )
+
+    for c in range(steps):
+        states_copy(c).start()
+    gram = jnp.zeros((RANK, RANK), f32)
+    for z in range(4):
+        gram = gram + dot(q_ref[z], q_ref[z], 1, 1)
+    total = jnp.sum(gram * square_ref[:, :RANK], keepdims=True)
+    scale = 1.0 / jnp.sqrt(total / (D * HID) + norm_eps)
+    q = q_ref[lax.axis_index("mp")]
+    both_ref[:RANK] = q
+    both_ref[RANK:] = q
+    q_out[...] = q.astype(f32)
+    start = pl.multiple_of(lax.axis_index("dp") * ROWS, ROWS)
+    decoded = dot(orth_ref[pl.ds(start, ROWS)], both_ref[...], 1, 0)
+    owned = adam(decoded * scale, master_ref[...], m_ref[...], v_ref[...])
+    small = [pltpu.make_async_copy(q_out, q_hbm, small_sems.at[3])]
+    for n, target in enumerate((m_hbm, v_hbm, master_hbm)):
+        owned_ref[n] = owned[n]
+        small.append(pltpu.make_async_copy(owned_ref.at[n], target, small_sems.at[n]))
+    for copy in small:
+        copy.start()
+
+    @pl.loop(0, steps)
+    def _(c):
+        rows = pl.ds(pl.multiple_of(c * BLOCK, BLOCK), BLOCK)
+        decoded = dot(orth_ref[rows], both_ref[...], 1, 0)
+        error_ref[rows] = merged_ref[rows] - decoded
+        update = decoded * scale
+        states_copy(c).wait()
+        for k in range(per):
+            state = [states_ref[c * per + k, n].astype(f32) for n in range(3)]
+            block = pl.ds(pl.multiple_of(c * BLOCK + k * ROWS, ROWS), ROWS)
+            weights_ref[block] = new_weights(update[k * ROWS : (k + 1) * ROWS], *state).astype(bf16)
+        for copy in out_copies(c):
+            copy.start()
+
+    for c in range(steps):
+        for copy in out_copies(c):
+            copy.wait()
+    for copy in small:
+        copy.wait()
 
 
 def final(q_all, orth, square, merged, states, master, m_state, v_state):
     steps = D // BLOCK
-    whole = lambda *shape: pl.BlockSpec(shape, lambda i: (0,) * len(shape))
     return pl.pallas_call(
         final_kernel,
-        grid=(steps,),
         out_shape=(
             jax.ShapeDtypeStruct((D, COLS), f32),
             jax.ShapeDtypeStruct((D, COLS), bf16),
-            jax.ShapeDtypeStruct((COLS, RANK), f32),
+            jax.ShapeDtypeStruct((RANK, COLS), f32),
             jax.ShapeDtypeStruct((ROWS, COLS), f32),
             jax.ShapeDtypeStruct((ROWS, COLS), f32),
             jax.ShapeDtypeStruct((ROWS, COLS), f32),
         ),
-        in_specs=[
-            whole(4, RANK, COLS),
-            whole(D, 2 * RANK),
-            whole(RANK, 2 * RANK),
-            pl.BlockSpec((BLOCK, COLS), lambda i: (i, 0)),
-            pl.BlockSpec((BLOCK // ROWS, 3, ROWS, COLS), lambda i: (i, 0, 0, 0)),
-            whole(ROWS, COLS),
-            whole(ROWS, COLS),
-            whole(ROWS, COLS),
+        in_specs=[pl.BlockSpec(memory_space=pltpu.VMEM)] * 4
+        + [pl.BlockSpec(memory_space=pltpu.HBM)]
+        + [pl.BlockSpec(memory_space=pltpu.VMEM)] * 3,
+        out_specs=(pl.BlockSpec(memory_space=pl.ANY),) * 6,
+        scratch_shapes=[
+            pltpu.VMEM((REPLICAS, 3, ROWS, COLS), bf16),
+            pltpu.VMEM((D, COLS), f32),
+            pltpu.VMEM((D, COLS), bf16),
+            pltpu.VMEM((RANK, COLS), f32),
+            pltpu.VMEM((3, ROWS, COLS), f32),
+            pltpu.VMEM((2 * RANK, COLS), bf16),
+            pltpu.SemaphoreType.DMA((steps,)),
+            pltpu.SemaphoreType.DMA((steps,)),
+            pltpu.SemaphoreType.DMA((steps,)),
+            pltpu.SemaphoreType.DMA((4,)),
         ],
-        out_specs=(
-            pl.BlockSpec((BLOCK, COLS), lambda i: (i, 0)),
-            pl.BlockSpec((BLOCK, COLS), lambda i: (i, 0)),
-            whole(COLS, RANK),
-            whole(ROWS, COLS),
-            whole(ROWS, COLS),
-            whole(ROWS, COLS),
-        ),
-        scratch_shapes=[pltpu.VMEM((2 * RANK, COLS), bf16), pltpu.VMEM((8, 128), f32)],
-        compiler_params=pltpu.CompilerParams(vmem_limit_bytes=VMEM_BYTES),
+        compiler_params=pltpu.CompilerParams(vmem_limit_bytes=32 * MIB),
         name="decode_update",
-    )(q_all, orth, square, merged, states, master, m_state, v_state)
+    )(q_all, orth, square, merged, hbm(states), master, m_state, v_state)
 
 
 def shards(grads, errors, q_init, master, m_state, v_state):
-    states = jnp.stack([master, m_state, v_state]).astype(bf16)
+    merged, part, states = left(grads, errors, q_init, master, m_state, v_state)
     states = lax.all_gather(states, "dp", axis=0, tiled=False)
-    merged, part = left(grads, errors, q_init)
     parts = lax.all_to_all(part.reshape(128, 8, 128), ("dp", "mp"), 0, 0)
     owned = sum_repeat(parts.reshape(HALF, 128))
     packed = lax.all_to_all(owned, ("dp", "mp"), 0, 0).reshape(HALF, 128)
@@ -300,7 +333,7 @@
     error_new, weights, q_new, master_new, m_new, v_new = final(
         q_all, orth, square, merged.reshape(D, COLS), states, master, m_state, v_state
     )
-    return (error_new[None], q_new, master_new, m_new, v_new, weights)
+    return (error_new[None], q_new.T, master_new, m_new, v_new, weights)
 
 
 def solution(mesh):

time: 123 us -> 113 us (0.919)
  blocking collectives: 72.6 us -> 66.8 us
  Pallas kernels: 28.8 us -> 24.1 us
  local copies, waits for them, and re-layouts: 4.57 us -> 7.94 us
  other arithmetic: 2.77 us -> 0.09 us
    pallas_call x1, Pallas kernels: 12.4 us -> 7.32 us  [final(): pl.pallas_call(final_kernel, out_shape=(jax.ShapeDtypeStruct((D, COLS), f...]
    unnamed x10 -> x12, local copies, waits for them, and re-layouts: 4.23 us -> 7.61 us
    pallas_call x1, Pallas kernels: 4.95 us -> 8.01 us  [left(): pl.pallas_call(left_kernel, out_shape=(jax.ShapeDtypeStruct((2, HALF, COL...]
    all_to_all x1, blocking collectives: 14 us -> 11.2 us  [shards(): q_parts = lax.all_to_all(q_part.reshape(32, 2, COLS), 'dp', 0, 0)]
    another operation x3 -> x0, other arithmetic: 2.68 us -> none  [shards(): states = jnp.stack([master, m_state, v_state]).astype(bf16)]
    pallas_call x1, Pallas kernels: 11.2 us -> 8.6 us  [right(): pl.pallas_call(right_kernel, out_shape=(jax.ShapeDtypeStruct((D, 2 * RANK...]
    all_to_all x1, blocking collectives: 20 us -> 17.9 us  [shards(): packed = lax.all_to_all(owned, ('dp', 'mp'), 0, 0).reshape(HALF, 128)]
  transfers between devices with their start and end apart: 1 -> 1, of which waited for: 0 -> 0; matrix products, arithmetic and copies ran while one was open for 1% -> 0% of each run, Pallas kernels for 13% -> 8%
where the time goes in v2:
time: 113 us
  blocking collectives  66.8 us (59%)
  Pallas kernels  24.1 us (21%)
  between operations  14.1 us (12%)
  local copies, waits for them, and re-layouts  7.94 us (7%)
    all_to_all x1, blocking collectives, shards(): parts = lax.all_to_all(part.reshape(128, 8, 128), ('dp', 'mp'), 0, 0)  22.4 us
    all_to_all x1, blocking collectives, shards(): packed = lax.all_to_all(owned, ('dp', 'mp'), 0, 0).reshape(HALF, 128)  17.9 us
    all_to_all x1, blocking collectives, shards(): q_all = lax.all_to_all(q_owned, ('mp', 'dp'), 0, 0).reshape(4, RANK, COLS)  15.2 us
    all_to_all x1, blocking collectives, shards(): q_parts = lax.all_to_all(q_part.reshape(32, 2, COLS), 'dp', 0, 0)  11.2 us
    pallas_call x1, Pallas kernels, right(): pl.pallas_call(right_kernel, out_shape=(jax.ShapeDtypeStruct((D, 2 * RANK...  8.6 us
    pallas_call x1, Pallas kernels, left(): pl.pallas_call(left_kernel, out_shape=(jax.ShapeDtypeStruct((2, HALF, COL...  8.01 us
    unnamed x12, local copies, waits for them, and re-layouts  7.61 us
    pallas_call x1, Pallas kernels, final(): pl.pallas_call(final_kernel, out_shape=(jax.ShapeDtypeStruct((D, COLS), f...  7.32 us
  transfers between devices with their start and end apart: 1, of which 0 were waited for; matrix products, arithmetic and copies ran while one was open for 0% of the time, Pallas kernels for 8%

profile of v2, /device:TPU:1, one launch (start us, length us, event | category | flops | bytes accessed | tf_op | source)
XLA Modules:
  0.0 113.1 jit_solution(5701261155748943295)
XLA Ops:
  7.2 0.0 all-gather.3.cloned.1.call-start
  7.2 8.0 %left_factor.1 = (f32[2,1024,640]{2,1,0:T(8,128)S(1)}, bf16[1024,128]{1,0:T(8,128)(2,1)S(1)}, bf16[3,64,640]{2,1,0:T(8,128)(2,1)}) custom-call(f32[2,1024,640]{2,1,0:T(8,128)} %bitcast.15, f32[2,1024,640]{2,1,0:T(8,128)} %bitcast.16, f32[64,640]{1,0:T(8,128)} %bitcast.17, f32[64,640]{1,0:T(8,128)} %master_ref.1, f32[64,640]{1,0:T(8,128)} %m_ref.1, ...), custom_call_target="tpu_custom_call" | custom-call | tf_op jit(solution)/shard_map/left_factor/pallas_call | solution.py:93
  15.2 0.0 copy-start
  15.2 2.3 %copy-done = f32[2,1024,640]{2,1,0:T(8,128)} copy-done((f32[2,1024,640]{2,1,0:T(8,128)}, f32[2,1024,640]{2,1,0:T(8,128)S(1)}, u32[]{:S(2)}) %copy-start) | copy-done | bytes 5242904
  17.6 0.0 copy-start.3
  17.6 0.0 copy-start.4
  17.6 0.0 copy-start.5
  17.6 0.0 all-gather.3.cloned.1.call-update
  17.6 22.4 %all_to_all.20 = bf16[128,8,128]{2,1,0:T(8,128)(2,1)S(1)} all-to-all(bf16[128,8,128]{2,1,0:T(8,128)(2,1)S(1)} %bitcast.13), channel_id=1, replica_groups=mesh['dp'=32,'mp'=4] {'dp','mp'}, dimensions={0} | all-to-all | bytes 524288 | tf_op jit(solution)/shard_map/all_to_all | solution.py:325
  40.0 0.2 sum_repeat.1
  40.2 17.9 %all_to_all.21 = f32[128,8,128]{2,1,0:T(8,128)S(1)} all-to-all(f32[128,8,128]{2,1,0:T(8,128)S(1)} %sum_repeat.1), channel_id=1, replica_groups=mesh['dp'=32,'mp'=4] {'dp','mp'}, dimensions={0} | all-to-all | bytes 1048576 | tf_op jit(solution)/shard_map/all_to_all | solution.py:327
  58.2 0.0 copy-start.1
  58.2 2.8 %copy-done.1 = f32[2,1024,640]{2,1,0:T(8,128)S(1)} copy-done((f32[2,1024,640]{2,1,0:T(8,128)S(1)}, f32[2,1024,640]{2,1,0:T(8,128)}, u32[]{:S(2)}) %copy-start.1) | copy-done | bytes 5242904
  60.9 8.6 %right_factor.1 = (bf16[2048,128]{1,0:T(8,128)(2,1)S(1)}, f32[64,128]{1,0:T(8,128)S(1)}, bf16[64,640]{1,0:T(8,128)(2,1)S(1)}) custom-call(f32[1024,128]{1,0:T(8,128)S(1)} %bitcast.11, f32[2,1024,640]{2,1,0:T(8,128)S(1)} %copy-done.1), custom_call_target="tpu_custom_call" | custom-call | tf_op jit(solution)/shard_map/right_factor/pallas_call | solution.py:193
  69.6 11.2 %all_to_all.22 = bf16[32,2,640]{2,1,0:T(2,128)(2,1)S(1)} all-to-all(bf16[32,2,640]{2,1,0:T(2,128)(2,1)S(1)} %reshape.42), channel_id=1, replica_groups=mesh['dp'=32,'mp'=4] {'dp'}, dimensions={0} | all-to-all | bytes 163840 | tf_op jit(solution)/shard_map/all_to_all | solution.py:329
  80.8 0.1 reduce_sum.12
  80.8 0.2 broadcast_in_dim.4
  81.0 15.2 %all_to_all.23 = bf16[128,2,640]{2,1,0:T(2,128)(2,1)S(1)} all-to-all(bf16[128,2,640]{2,1,0:T(2,128)(2,1)S(1)} %broadcast_in_dim.4), channel_id=1, replica_groups=mesh['dp'=32,'mp'=4] {'mp','dp'}, dimensions={0} | all-to-all | bytes 655360 | tf_op jit(solution)/shard_map/all_to_all | solution.py:332
  96.2 0.1 reshape.43.q_ref
  96.4 0.0 all-gather.3.cloned.1.call-done
  96.4 0.0 copy-done.3
  96.4 0.0 copy-done.4
  96.4 0.0 copy-done.5
  96.4 0.0 copy-start.2
  96.4 2.5 %copy-done.2 = f32[2,1024,640]{2,1,0:T(8,128)S(1)} copy-done((f32[2,1024,640]{2,1,0:T(8,128)S(1)}, f32[2,1024,640]{2,1,0:T(8,128)}, u32[]{:S(2)}) %copy-start.2) | copy-done | bytes 5242904
  98.9 7.3 %decode_update.1 = (f32[2048,640]{1,0:T(8,128)}, bf16[2048,640]{1,0:T(8,128)(2,1)}, f32[64,640]{1,0:T(8,128)}, f32[64,640]{1,0:T(8,128)}, f32[64,640]{1,0:T(8,128)}, /*index=5*/f32[64,640]{1,0:T(8,128)}) custom-call(bf16[4,64,640]{2,1,0:T(8,128)(2,1)S(1)} %reshape.43.q_ref, bf16[2048,128]{1,0:T(8,128)(2,1)S(1)} %get-tuple-element.21.orth_ref, ...), custom_call_target="tpu_custom_call" | custom-call | tf_op jit(solution)/shard_map/decode_update/pallas_call | solution.py:291
  (1 shorter events, 0.0 us)
Async XLA Ops:
  7.2 89.2 %all-gather.3.cloned.1.call-start = ((), (), s32[]{:S(2)}) async-start(), calls=%async_computation.4 | async-start | bytes 8110080 | tf_op jit(solution)/shard_map/all_gather | solution.py:324
  15.2 2.4 %copy-start = (f32[2,1024,640]{2,1,0:T(8,128)}, f32[2,1024,640]{2,1,0:T(8,128)S(1)}, u32[]{:S(2)}) copy-start(f32[2,1024,640]{2,1,0:T(8,128)S(1)} %get-tuple-element.19.merged_ref) | copy-start | bytes 15728644
  17.6 78.8 %copy-start.3 = (f32[64,640]{1,0:T(8,128)S(1)}, f32[64,640]{1,0:T(8,128)}, u32[]{:S(2)}) copy-start(f32[64,640]{1,0:T(8,128)} %master_ref.1) | copy-start | bytes 491524
  17.6 78.8 %copy-start.4 = (f32[64,640]{1,0:T(8,128)S(1)}, f32[64,640]{1,0:T(8,128)}, u32[]{:S(2)}) copy-start(f32[64,640]{1,0:T(8,128)} %m_ref.1) | copy-start | bytes 491524
  17.6 78.8 %copy-start.5 = (f32[64,640]{1,0:T(8,128)S(1)}, f32[64,640]{1,0:T(8,128)}, u32[]{:S(2)}) copy-start(f32[64,640]{1,0:T(8,128)} %v_ref.1) | copy-start | bytes 491524
  58.2 2.8 %copy-start.1 = (f32[2,1024,640]{2,1,0:T(8,128)S(1)}, f32[2,1024,640]{2,1,0:T(8,128)}, u32[]{:S(2)}) copy-start(f32[2,1024,640]{2,1,0:T(8,128)} %copy-done) | copy-start | bytes 15728644
  96.4 2.5 %copy-start.2 = (f32[2,1024,640]{2,1,0:T(8,128)S(1)}, f32[2,1024,640]{2,1,0:T(8,128)}, u32[]{:S(2)}) copy-start(f32[2,1024,640]{2,1,0:T(8,128)} %copy-done) | copy-start | bytes 15728644
Sparse Core Ops, SparseCore 0:
  17.7 55.6 all-gather.2

commit v3 on v2

--- a/solution.py
+++ b/solution.py
@@ -26,6 +26,7 @@
 HIGHEST = lax.Precision.HIGHEST
 MIB = 1024 * 1024
 LEFT_CHUNKS = 8
+AHEAD = 3
 BLOCK = 256
 
 
@@ -50,8 +51,8 @@
 
 def left_kernel(
     grads, errors, q_hbm, master, m_state, v_state,
-    merged_ref, part_ref, states_ref,
-    buffer, q_buffer, state_buffer, sems, small_sems,
+    merged_hbm, part_ref, states_hbm,
+    merged_ref, buffer, q_buffer, state_buffer, states_ref, sems, out_sems, small_sems,
 ):
     size = HALF // LEFT_CHUNKS
     small = [pltpu.make_async_copy(q_hbm, q_buffer, small_sems.at[0])]
@@ -66,9 +67,9 @@
             pltpu.make_async_copy(grads.at[:, rows], merged_ref.at[:, rows], sems.at[0, c]),
             pltpu.make_async_copy(errors.at[:, rows], buffer.at[:, rows], sems.at[1, c]),
         )
-        for copy in pair:
-            copy.start()
         copies.append(pair)
+    for copy in sum(copies[:AHEAD], ()):
+        copy.start()
     small[0].wait()
     q = q_buffer[...]
     q_high = q.astype(bf16).astype(f32)
@@ -76,35 +77,51 @@
     for n in range(3):
         small[n + 1].wait()
         states_ref[n] = state_buffer[n].astype(bf16)
+    outs = [pltpu.make_async_copy(states_ref, states_hbm, small_sems.at[4])]
+    outs[0].start()
     low_lanes = lanes((size, 2 * RANK)) < RANK
     for c in range(LEFT_CHUNKS):
         for copy in copies[c]:
             copy.wait()
+        for copy in sum(copies[c + AHEAD : c + AHEAD + 1], ()):
+            copy.start()
         rows = pl.ds(c * size, size)
         merged = merged_ref[:, rows] + buffer[:, rows]
         merged_ref[:, rows] = merged
-        high, low = split(merged.reshape(2 * size, COLS))
-        part = dot(high, right, 1, 0) + dot(low, right, 1, 0)
+        outs.append(
+            pltpu.make_async_copy(merged_ref.at[:, rows], merged_hbm.at[:, rows], out_sems.at[c])
+        )
+        outs[-1].start()
+        part = dot(merged.reshape(2 * size, COLS).astype(bf16), right, 1, 0)
         part = part + pltpu.roll(part, RANK, 1)
         part_ref[rows, :] = jnp.where(low_lanes, part[:size], part[size:]).astype(bf16)
+    for copy in outs:
+        copy.wait()
 
 
 def left(grads, errors, q_init, master, m_state, v_state):
     return pl.pallas_call(
         left_kernel,
         out_shape=(
-            jax.ShapeDtypeStruct((2, HALF, COLS), f32),
+            pltpu.HBM((2, HALF, COLS), f32),
             jax.ShapeDtypeStruct((HALF, 2 * RANK), bf16),
-            jax.ShapeDtypeStruct((3, ROWS, COLS), bf16),
+            pltpu.HBM((3, ROWS, COLS), bf16),
         ),
         in_specs=[pl.BlockSpec(memory_space=pltpu.HBM)] * 6,
-        out_specs=(pl.BlockSpec(memory_space=pltpu.VMEM),) * 3,
+        out_specs=(
+            pl.BlockSpec(memory_space=pltpu.HBM),
+            pl.BlockSpec(memory_space=pltpu.VMEM),
+            pl.BlockSpec(memory_space=pltpu.HBM),
+        ),
         scratch_shapes=[
+            pltpu.VMEM((2, HALF, COLS), f32),
             pltpu.VMEM((2, HALF, COLS), f32),
             pltpu.VMEM((RANK, COLS), f32),
             pltpu.VMEM((3, ROWS, COLS), f32),
+            pltpu.VMEM((3, ROWS, COLS), bf16),
             pltpu.SemaphoreType.DMA((2, LEFT_CHUNKS)),
-            pltpu.SemaphoreType.DMA((4,)),
+            pltpu.SemaphoreType.DMA((LEFT_CHUNKS,)),
+            pltpu.SemaphoreType.DMA((5,)),
         ],
         compiler_params=pltpu.CompilerParams(vmem_limit_bytes=20 * MIB),
         name="left_factor",
@@ -130,24 +147,35 @@
     )(parts)
 
 
-def inverse_factor(gram):
+def inverse_factor(gram, after_panel):
     row_id = lax.broadcasted_iota(jnp.int32, (RANK, 2 * RANK), 0)
     lane = lanes((RANK, 2 * RANK))
     eye = jnp.where(row_id == lane, 1.0, 0.0).astype(f32)
     trace = jnp.sum(gram * eye, keepdims=True)
     jitter = 1e-06 * trace / RANK + 1e-06
     start = jnp.where(lane < RANK, gram + jitter * eye, jnp.where(row_id == lane - RANK, 1.0, 0.0))
-    tiles = [start[8 * k : 8 * k + 8] for k in range(RANK // 8)]
-    sub = lax.broadcasted_iota(jnp.int32, (8, 1), 0)
-    for j in range(RANK - 1):
-        t, r = divmod(j, 8)
-        row = tiles[t][r : r + 1]
-        row = row * (1.0 / row[:, j : j + 1])
-        for k in range(t, RANK // 8):
-            factor = tiles[k][:, j : j + 1]
-            if k == t:
-                factor = jnp.where(sub > r, factor, 0.0)
-            tiles[k] = tiles[k] - factor * row
+    count = RANK // 8
+    tiles = [start[8 * k : 8 * k + 8] for k in range(count)]
+    sub = lax.broadcasted_iota(jnp.int32, (8, 2 * RANK), 0)
+    for t in range(count):
+        below = range(t, count)
+        columns = {
+            (c, k): jnp.broadcast_to(tiles[k][:, 8 * t + c : 8 * t + c + 1], sub.shape)
+            for c in range(8)
+            for k in below
+        }
+        for c in range(8):
+            reciprocal = 1.0 / columns[c, t][c : c + 1]
+            factors = {k: columns[c, k] * reciprocal for k in below}
+            factors[t] = jnp.where(sub > c, factors[t], 0.0)
+            for later in range(c + 1, 8):
+                pivot_row = columns[later, t][c : c + 1]
+                for k in below:
+                    columns[later, k] = columns[later, k] - factors[k] * pivot_row
+            pivot_row = tiles[t][c : c + 1]
+            for k in below:
+                tiles[k] = tiles[k] - factors[k] * pivot_row
+        after_panel(t)
     done = jnp.concatenate(tiles, axis=0)
     pivots = jnp.sum(done * eye, axis=1, keepdims=True)
     return jnp.where(lane < RANK, 0.0, done * (1.0 / jnp.sqrt(pivots)))
@@ -162,31 +190,52 @@
     return top, bottom
 
 
-def right_kernel(p_ref, merged_ref, orth_ref, square_ref, part_ref):
-    packed = p_ref[...]
-    gram = dot(packed, packed, 0, 0, HIGHEST)
-    shifted = pltpu.roll(gram[RANK:], RANK, 1)
-    gram = gram[:RANK] + shifted
-    inverse = inverse_factor(gram)
-
-    pairs = pair_rows(packed)
-    acc = jnp.zeros((2 * RANK, COLS), f32)
+def pair_gram(halves):
+    square = sum(dot(half, half, 0, 0) for half in halves)
+    square = square[:RANK] + square[RANK:]
+    return square + pltpu.roll(square, RANK, 1)
+
+
+def right_kernel(p_ref, merged_hbm, orth_ref, square_ref, part_ref, merged_ref, sems):
+    def copy(c):
+        half, rows = c // 4, pl.ds(c % 4 * BLOCK, BLOCK)
+        return pltpu.make_async_copy(
+            merged_hbm.at[half, rows], merged_ref.at[half, rows], sems.at[c]
+        )
+
+    for c in range(AHEAD):
+        copy(c).start()
+    pairs = pair_rows(p_ref[...])
+    acc = [jnp.zeros((2 * RANK, COLS), f32)]
+
+    def multiply(c):
+        copy(c).wait()
+        if c + AHEAD < D // BLOCK:
+            copy(c + AHEAD).start()
+        half, rows = c // 4, pl.ds(c % 4 * BLOCK, BLOCK)
+        left = pairs[half][c % 4 * BLOCK : (c % 4 + 1) * BLOCK]
+        acc[0] = acc[0] + dot(left, merged_ref[half, rows].astype(bf16), 0, 0)
+
+    inverse = inverse_factor(pair_gram(pairs), multiply)
+    part = acc[0][:RANK] + acc[0][RANK:]
+
+    flipped = pltpu.roll(inverse, RANK, 1)
+    inverse_small = flipped[:, :RANK]
+    part_ref[...] = (dot(inverse_small, part, 1, 0, HIGHEST) * (1.0 / REPLICAS)).astype(bf16)
+
+    high = inverse_small.astype(bf16).astype(f32)
+    factor = jnp.concatenate([high, inverse_small - high], axis=0).T
+    factor = jnp.concatenate([factor, factor], axis=0).astype(bf16)
+    halves = []
+    low_lanes = lanes((HALF, 2 * RANK)) < RANK
     for half in range(2):
-        for c in range(4):
-            rows = slice(c * BLOCK, (c + 1) * BLOCK)
-            high, low = split(merged_ref[half, rows])
-            acc = acc + (dot(pairs[half][rows], high, 0, 0) + dot(pairs[half][rows], low, 0, 0))
-    part = acc[:RANK] + acc[RANK:]
-
-    both = jnp.concatenate([pltpu.roll(inverse, RANK, 1), inverse], axis=0)
-    inverse_small = both[:RANK, :RANK]
-    part_ref[...] = (dot(inverse_small, part, 1, 0, HIGHEST) * (1.0 / REPLICAS)).astype(bf16)
-    orth = dot(packed, both, 1, 1, HIGHEST)
-    square = dot(orth, orth, 0, 0, HIGHEST)
-    square_ref[...] = square[:RANK] + pltpu.roll(square[RANK:], RANK, 1)
-    top, bottom = pair_rows(orth)
-    orth_ref[:HALF] = top
-    orth_ref[HALF:] = bottom
+        orth = dot(pairs[half], factor, 1, 0)
+        orth = orth + pltpu.roll(orth, RANK, 1)
+        high = orth.astype(bf16).astype(f32)
+        pair = jnp.where(low_lanes, high, orth - high).astype(bf16)
+        orth_ref[half * HALF : (half + 1) * HALF] = pair
+        halves.append(pair)
+    square_ref[...] = pair_gram(halves)
 
 
 def right(packed, merged):
@@ -197,11 +246,18 @@
             jax.ShapeDtypeStruct((RANK, 2 * RANK), f32),
             jax.ShapeDtypeStruct((RANK, COLS), bf16),
         ),
-        in_specs=[pl.BlockSpec(memory_space=pltpu.VMEM)] * 2,
+        in_specs=[
+            pl.BlockSpec(memory_space=pltpu.VMEM),
+            pl.BlockSpec(memory_space=pltpu.HBM),
+        ],
         out_specs=(pl.BlockSpec(memory_space=pltpu.VMEM),) * 3,
+        scratch_shapes=[
+            pltpu.VMEM((2, HALF, COLS), f32),
+            pltpu.SemaphoreType.DMA((D // BLOCK,)),
+        ],
         compiler_params=pltpu.CompilerParams(vmem_limit_bytes=16 * MIB),
         name="right_factor",
-    )(packed, merged)
+    )(packed, hbm(merged))
 
 
 def adam(update, master, m_state, v_state):
@@ -225,10 +281,10 @@
 
 
 def final_kernel(
-    q_ref, orth_ref, square_ref, merged_ref, states_hbm, master_ref, m_ref, v_ref,
+    q_ref, orth_ref, square_ref, merged_hbm, states_hbm, master_ref, m_ref, v_ref,
     error_hbm, weights_hbm, q_hbm, master_hbm, m_hbm, v_hbm,
-    states_ref, error_ref, weights_ref, q_out, owned_ref, both_ref,
-    in_sems, error_sems, weight_sems, small_sems,
+    states_ref, merged_ref, error_ref, weights_ref, q_out, owned_ref, both_ref,
+    in_sems, merged_sems, error_sems, weight_sems, small_sems,
 ):
     steps = D // BLOCK
     per = BLOCK // ROWS
@@ -236,6 +292,14 @@
     def states_copy(c):
         part = pl.ds(c * per, per)
         return pltpu.make_async_copy(states_hbm.at[part], states_ref.at[part], in_sems.at[c])
+
+    def merged_copy(c):
+        half = c // (steps // 2)
+        rows = pl.ds(pl.multiple_of((c - half * (steps // 2)) * BLOCK, BLOCK), BLOCK)
+        whole = pl.ds(pl.multiple_of(c * BLOCK, BLOCK), BLOCK)
+        return pltpu.make_async_copy(
+            merged_hbm.at[half, rows], merged_ref.at[whole], merged_sems.at[c]
+        )
 
     def out_copies(c):
         rows = pl.ds(pl.multiple_of(c * BLOCK, BLOCK), BLOCK)
@@ -244,7 +308,8 @@
             pltpu.make_async_copy(weights_ref.at[rows], weights_hbm.at[rows], weight_sems.at[c]),
         )
 
-    for c in range(steps):
+    for c in range(AHEAD):
+        merged_copy(c).start()
         states_copy(c).start()
     gram = jnp.zeros((RANK, RANK), f32)
     for z in range(4):
@@ -269,6 +334,13 @@
     def _(c):
         rows = pl.ds(pl.multiple_of(c * BLOCK, BLOCK), BLOCK)
         decoded = dot(orth_ref[rows], both_ref[...], 1, 0)
+        merged_copy(c).wait()
+
+        @pl.when(c + AHEAD < steps)
+        def _():
+            merged_copy(c + AHEAD).start()
+            states_copy(c + AHEAD).start()
+
         error_ref[rows] = merged_ref[rows] - decoded
         update = decoded * scale
         states_copy(c).wait()
@@ -298,12 +370,13 @@
             jax.ShapeDtypeStruct((ROWS, COLS), f32),
             jax.ShapeDtypeStruct((ROWS, COLS), f32),
         ),
-        in_specs=[pl.BlockSpec(memory_space=pltpu.VMEM)] * 4
-        + [pl.BlockSpec(memory_space=pltpu.HBM)]
+        in_specs=[pl.BlockSpec(memory_space=pltpu.VMEM)] * 3
+        + [pl.BlockSpec(memory_space=pltpu.HBM)] * 2
         + [pl.BlockSpec(memory_space=pltpu.VMEM)] * 3,
         out_specs=(pl.BlockSpec(memory_space=pl.ANY),) * 6,
         scratch_shapes=[
             pltpu.VMEM((REPLICAS, 3, ROWS, COLS), bf16),
+            pltpu.VMEM((D, COLS), f32),
             pltpu.VMEM((D, COLS), f32),
             pltpu.VMEM((D, COLS), bf16),
             pltpu.VMEM((RANK, COLS), f32),
@@ -312,11 +385,12 @@
             pltpu.SemaphoreType.DMA((steps,)),
             pltpu.SemaphoreType.DMA((steps,)),
             pltpu.SemaphoreType.DMA((steps,)),
+            pltpu.SemaphoreType.DMA((steps,)),
             pltpu.SemaphoreType.DMA((4,)),
         ],
         compiler_params=pltpu.CompilerParams(vmem_limit_bytes=32 * MIB),
         name="decode_update",
-    )(q_all, orth, square, merged, hbm(states), master, m_state, v_state)
+    )(q_all, orth, square, hbm(merged), hbm(states), master, m_state, v_state)
 
 
 def shards(grads, errors, q_init, master, m_state, v_state):
@@ -331,7 +405,7 @@
     q_owned = jnp.broadcast_to(q_owned[None], (128, 2, COLS))
     q_all = lax.all_to_all(q_owned, ("mp", "dp"), 0, 0).reshape(4, RANK, COLS)
     error_new, weights, q_new, master_new, m_new, v_new = final(
-        q_all, orth, square, merged.reshape(D, COLS), states, master, m_state, v_state
+        q_all, orth, square, merged, states, master, m_state, v_state
     )
     return (error_new[None], q_new.T, master_new, m_new, v_new, weights)
 

time: 113 us -> 105 us (0.929)
  local copies, waits for them, and re-layouts: 7.94 us -> 0.35 us
  Pallas kernels: 24.1 us -> 22 us
    unnamed x12 -> x6, local copies, waits for them, and re-layouts: 7.61 us -> 0.02 us
    pallas_call x1, Pallas kernels: 8.6 us -> 5.09 us  [right(): pl.pallas_call(right_kernel, out_shape=(jax.ShapeDtypeStruct((D, 2 * RANK...]
    pallas_call x1, Pallas kernels: 7.32 us -> 8.86 us  [final(): pl.pallas_call(final_kernel, out_shape=(jax.ShapeDtypeStruct((D, COLS), f...]
  transfers between devices with their start and end apart: 1 -> 1, of which waited for: 0 -> 0; matrix products, arithmetic and copies ran while one was open for 0% -> 0% of each run, Pallas kernels for 8% -> 5%
where the time goes in v3:
time: 105 us; the launch traced here: 104 us
  blocking collectives  67.8 us (65%)
  Pallas kernels  22 us (21%)
  between operations  14.1 us (13%)
    all_to_all x1, blocking collectives, shards(): parts = lax.all_to_all(part.reshape(128, 8, 128), ('dp', 'mp'), 0, 0)  22.4 us
    all_to_all x1, blocking collectives, shards(): packed = lax.all_to_all(owned, ('dp', 'mp'), 0, 0).reshape(HALF, 128)  17.9 us
    all_to_all x1, blocking collectives, shards(): q_all = lax.all_to_all(q_owned, ('mp', 'dp'), 0, 0).reshape(4, RANK, COLS)  16.1 us
    all_to_all x1, blocking collectives, shards(): q_parts = lax.all_to_all(q_part.reshape(32, 2, COLS), 'dp', 0, 0)  11.3 us
    pallas_call x1, Pallas kernels, final(): pl.pallas_call(final_kernel, out_shape=(jax.ShapeDtypeStruct((D, COLS), f...  8.86 us
    pallas_call x1, Pallas kernels, left(): pl.pallas_call(left_kernel, out_shape=(pltpu.HBM((2, HALF, COLS), f32), j...  7.87 us
    pallas_call x1, Pallas kernels, right(): pl.pallas_call(right_kernel, out_shape=(jax.ShapeDtypeStruct((D, 2 * RANK...  5.09 us
  transfers between devices with their start and end apart: 1, of which 0 were waited for; matrix products, arithmetic and copies ran while one was open for 0% of the time, Pallas kernels for 5%

profile of v3, /device:TPU:1, one launch (start us, length us, event | category | flops | bytes accessed | tf_op | source)
XLA Modules:
  0.0 104.4 jit_solution(2467326344596326187)
XLA Ops:
  7.2 0.0 all-gather.3.cloned.1.call-start
  7.2 7.9 %left_factor.1 = (f32[2,1024,640]{2,1,0:T(8,128)}, bf16[1024,128]{1,0:T(8,128)(2,1)S(1)}, bf16[3,64,640]{2,1,0:T(8,128)(2,1)}) custom-call(f32[2,1024,640]{2,1,0:T(8,128)} %bitcast.13, f32[2,1024,640]{2,1,0:T(8,128)} %bitcast.14, f32[64,640]{1,0:T(8,128)} %bitcast.15, f32[64,640]{1,0:T(8,128)} %master_ref.1, f32[64,640]{1,0:T(8,128)} %m_ref.1, f32[64,640]{1,0:T(8,128)} %v_ref.1), custom_call_target="tpu_custom_call" | custom-call | tf_op jit(solution)/shard_map/left_factor/pallas_call | solution.py:103
  15.1 0.0 copy-start
  15.1 0.0 copy-start.1
  15.1 0.0 copy-start.2
  15.1 0.0 all-gather.3.cloned.1.call-update
  15.2 22.4 %all_to_all.20 = bf16[128,8,128]{2,1,0:T(8,128)(2,1)S(1)} all-to-all(bf16[128,8,128]{2,1,0:T(8,128)(2,1)S(1)} %bitcast.11), channel_id=1, replica_groups=mesh['dp'=32,'mp'=4] {'dp','mp'}, dimensions={0} | all-to-all | bytes 524288 | tf_op jit(solution)/shard_map/all_to_all | solution.py:399
  37.6 0.2 sum_repeat.1
  37.8 17.9 %all_to_all.21 = f32[128,8,128]{2,1,0:T(8,128)S(1)} all-to-all(f32[128,8,128]{2,1,0:T(8,128)S(1)} %sum_repeat.1), channel_id=1, replica_groups=mesh['dp'=32,'mp'=4] {'dp','mp'}, dimensions={0} | all-to-all | bytes 1048576 | tf_op jit(solution)/shard_map/all_to_all | solution.py:401
  55.7 5.1 %right_factor.1 = (bf16[2048,128]{1,0:T(8,128)(2,1)S(1)}, f32[64,128]{1,0:T(8,128)S(1)}, bf16[64,640]{1,0:T(8,128)(2,1)S(1)}) custom-call(f32[1024,128]{1,0:T(8,128)S(1)} %bitcast.9, f32[2,1024,640]{2,1,0:T(8,128)} %get-tuple-element.19.merged_hbm), custom_call_target="tpu_custom_call" | custom-call | tf_op jit(solution)/shard_map/right_factor/pallas_call | solution.py:242
  60.8 11.3 %all_to_all.22 = bf16[32,2,640]{2,1,0:T(2,128)(2,1)S(1)} all-to-all(bf16[32,2,640]{2,1,0:T(2,128)(2,1)S(1)} %reshape.39), channel_id=1, replica_groups=mesh['dp'=32,'mp'=4] {'dp'}, dimensions={0} | all-to-all | bytes 163840 | tf_op jit(solution)/shard_map/all_to_all | solution.py:403
  72.1 0.1 reduce_sum.12
  72.2 0.2 broadcast_in_dim.4
  72.4 16.1 %all_to_all.23 = bf16[128,2,640]{2,1,0:T(2,128)(2,1)S(1)} all-to-all(bf16[128,2,640]{2,1,0:T(2,128)(2,1)S(1)} %broadcast_in_dim.4), channel_id=1, replica_groups=mesh['dp'=32,'mp'=4] {'mp','dp'}, dimensions={0} | all-to-all | bytes 655360 | tf_op jit(solution)/shard_map/all_to_all | solution.py:406
  88.5 0.1 reshape.40.q_ref
  88.6 0.0 all-gather.3.cloned.1.call-done
  88.7 0.0 copy-done
  88.7 0.0 copy-done.1
  88.7 0.0 copy-done.2
  88.7 8.9 %decode_update.1 = (f32[2048,640]{1,0:T(8,128)}, bf16[2048,640]{1,0:T(8,128)(2,1)}, f32[64,640]{1,0:T(8,128)}, f32[64,640]{1,0:T(8,128)}, f32[64,640]{1,0:T(8,128)}, /*index=5*/f32[64,640]{1,0:T(8,128)}) custom-call(bf16[4,64,640]{2,1,0:T(8,128)(2,1)S(1)} %reshape.40.q_ref, bf16[2048,128]{1,0:T(8,128)(2,1)S(1)} %get-tuple-element.21.orth_ref, ...), custom_call_target="tpu_custom_call" | custom-call | tf_op jit(solution)/shard_map/decode_update/pallas_call | solution.py:363
  (1 shorter events, 0.0 us)
Async XLA Ops:
  7.2 81.5 %all-gather.3.cloned.1.call-start = ((), (), s32[]{:S(2)}) async-start(), calls=%async_computation.4 | async-start | bytes 8110080 | tf_op jit(solution)/shard_map/all_gather | solution.py:398
  15.1 73.6 %copy-start = (f32[64,640]{1,0:T(8,128)S(1)}, f32[64,640]{1,0:T(8,128)}, u32[]{:S(2)}) copy-start(f32[64,640]{1,0:T(8,128)} %master_ref.1) | copy-start | bytes 491524
  15.1 73.6 %copy-start.1 = (f32[64,640]{1,0:T(8,128)S(1)}, f32[64,640]{1,0:T(8,128)}, u32[]{:S(2)}) copy-start(f32[64,640]{1,0:T(8,128)} %m_ref.1) | copy-start | bytes 491524
  15.1 73.6 %copy-start.2 = (f32[64,640]{1,0:T(8,128)S(1)}, f32[64,640]{1,0:T(8,128)}, u32[]{:S(2)}) copy-start(f32[64,640]{1,0:T(8,128)} %v_ref.1) | copy-start | bytes 491524
Sparse Core Ops, SparseCore 0:
  15.3 56.3 all-gather.2

commit v4 on v3

--- a/solution.py
+++ b/solution.py
@@ -26,13 +26,10 @@
 HIGHEST = lax.Precision.HIGHEST
 MIB = 1024 * 1024
 LEFT_CHUNKS = 8
-AHEAD = 3
+AHEAD = 5
+DELAY = 2
+RIGHT_AHEAD = 3
 BLOCK = 256
-
-
-def split(x):
-    high = x.astype(bf16)
-    return high, (x - high.astype(f32)).astype(bf16)
 
 
 def dot(a, b, ca, cb, precision=None):
@@ -58,8 +55,7 @@
     small = [pltpu.make_async_copy(q_hbm, q_buffer, small_sems.at[0])]
     for n, source in enumerate((master, m_state, v_state)):
         small.append(pltpu.make_async_copy(source, state_buffer.at[n], small_sems.at[n + 1]))
-    for copy in small:
-        copy.start()
+    small[0].start()
     copies = []
     for c in range(LEFT_CHUNKS):
         rows = pl.ds(c * size, size)
@@ -67,34 +63,43 @@
             pltpu.make_async_copy(grads.at[:, rows], merged_ref.at[:, rows], sems.at[0, c]),
             pltpu.make_async_copy(errors.at[:, rows], buffer.at[:, rows], sems.at[1, c]),
         )
+        for copy in pair:
+            copy.start()
         copies.append(pair)
-    for copy in sum(copies[:AHEAD], ()):
+    for copy in small[1:]:
         copy.start()
-    small[0].wait()
-    q = q_buffer[...]
-    q_high = q.astype(bf16).astype(f32)
-    right = jnp.concatenate([q_high, q - q_high], axis=0).T.astype(bf16)
-    for n in range(3):
-        small[n + 1].wait()
-        states_ref[n] = state_buffer[n].astype(bf16)
-    outs = [pltpu.make_async_copy(states_ref, states_hbm, small_sems.at[4])]
-    outs[0].start()
     low_lanes = lanes((size, 2 * RANK)) < RANK
-    for c in range(LEFT_CHUNKS):
-        for copy in copies[c]:
-            copy.wait()
-        for copy in sum(copies[c + AHEAD : c + AHEAD + 1], ()):
-            copy.start()
-        rows = pl.ds(c * size, size)
-        merged = merged_ref[:, rows] + buffer[:, rows]
-        merged_ref[:, rows] = merged
-        outs.append(
-            pltpu.make_async_copy(merged_ref.at[:, rows], merged_hbm.at[:, rows], out_sems.at[c])
-        )
-        outs[-1].start()
-        part = dot(merged.reshape(2 * size, COLS).astype(bf16), right, 1, 0)
-        part = part + pltpu.roll(part, RANK, 1)
-        part_ref[rows, :] = jnp.where(low_lanes, part[:size], part[size:]).astype(bf16)
+    outs = []
+    right = None
+    for c in range(LEFT_CHUNKS + DELAY):
+        if c < LEFT_CHUNKS:
+            rows = pl.ds(c * size, size)
+            for copy in copies[c]:
+                copy.wait()
+            merged_ref[:, rows] = merged_ref[:, rows] + buffer[:, rows]
+            outs.append(
+                pltpu.make_async_copy(
+                    merged_ref.at[:, rows], merged_hbm.at[:, rows], out_sems.at[c]
+                )
+            )
+            outs[-1].start()
+        if c == DELAY:
+            small[0].wait()
+            q = q_buffer[...]
+            q_high = q.astype(bf16).astype(f32)
+            right = jnp.concatenate([q_high, q - q_high], axis=0).T.astype(bf16)
+        if c == LEFT_CHUNKS - 1:
+            for n in range(3):
+                small[n + 1].wait()
+                states_ref[n] = state_buffer[n].astype(bf16)
+            outs.append(pltpu.make_async_copy(states_ref, states_hbm, small_sems.at[4]))
+            outs[-1].start()
+        if c >= DELAY:
+            rows = pl.ds((c - DELAY) * size, size)
+            merged = merged_ref[:, rows].reshape(2 * size, COLS).astype(bf16)
+            part = dot(merged, right, 1, 0)
+            part = part + pltpu.roll(part, RANK, 1)
+            part_ref[rows, :] = jnp.where(low_lanes, part[:size], part[size:]).astype(bf16)
     for copy in outs:
         copy.wait()
 
@@ -203,15 +208,15 @@
             merged_hbm.at[half, rows], merged_ref.at[half, rows], sems.at[c]
         )
 
-    for c in range(AHEAD):
+    for c in range(RIGHT_AHEAD):
         copy(c).start()
     pairs = pair_rows(p_ref[...])
     acc = [jnp.zeros((2 * RANK, COLS), f32)]
 
     def multiply(c):
         copy(c).wait()
-        if c + AHEAD < D // BLOCK:
-            copy(c + AHEAD).start()
+        if c + RIGHT_AHEAD < D // BLOCK:
+            copy(c + RIGHT_AHEAD).start()
         half, rows = c // 4, pl.ds(c % 4 * BLOCK, BLOCK)
         left = pairs[half][c % 4 * BLOCK : (c % 4 + 1) * BLOCK]
         acc[0] = acc[0] + dot(left, merged_ref[half, rows].astype(bf16), 0, 0)

time: 105 us -> 104 us (level)
  no operation moved by 1% of the time
where the time goes in v4:
time: 104 us; the launch traced here: 103 us
  blocking collectives  67.8 us (65%)
  Pallas kernels  21 us (20%)
  between operations  14.1 us (14%)
    all_to_all x1, blocking collectives, shards(): parts = lax.all_to_all(part.reshape(128, 8, 128), ('dp', 'mp'), 0, 0)  22.4 us
    all_to_all x1, blocking collectives, shards(): packed = lax.all_to_all(owned, ('dp', 'mp'), 0, 0).reshape(HALF, 128)  17.9 us
    all_to_all x1, blocking collectives, shards(): q_all = lax.all_to_all(q_owned, ('mp', 'dp'), 0, 0).reshape(4, RANK, COLS)  16.1 us
    all_to_all x1, blocking collectives, shards(): q_parts = lax.all_to_all(q_part.reshape(32, 2, COLS), 'dp', 0, 0)  11.3 us
    pallas_call x1, Pallas kernels, final(): pl.pallas_call(final_kernel, out_shape=(jax.ShapeDtypeStruct((D, COLS), f...  8.57 us
    pallas_call x1, Pallas kernels, left(): pl.pallas_call(left_kernel, out_shape=(pltpu.HBM((2, HALF, COLS), f32), j...  7.15 us
    pallas_call x1, Pallas kernels, right(): pl.pallas_call(right_kernel, out_shape=(jax.ShapeDtypeStruct((D, 2 * RANK...  5.08 us
  transfers between devices with their start and end apart: 1, of which 0 were waited for; matrix products, arithmetic and copies ran while one was open for 0% of the time, Pallas kernels for 5%

profile of v4, /device:TPU:1, one launch (start us, length us, event | category | flops | bytes accessed | tf_op | source)
XLA Modules:
  0.0 103.4 jit_solution(9157370657767842889)
XLA Ops:
  7.2 0.0 all-gather.3.cloned.1.call-start
  7.2 7.2 %left_factor.1 = (f32[2,1024,640]{2,1,0:T(8,128)}, bf16[1024,128]{1,0:T(8,128)(2,1)S(1)}, bf16[3,64,640]{2,1,0:T(8,128)(2,1)}) custom-call(f32[2,1024,640]{2,1,0:T(8,128)} %bitcast.13, f32[2,1024,640]{2,1,0:T(8,128)} %bitcast.14, f32[64,640]{1,0:T(8,128)} %bitcast.15, f32[64,640]{1,0:T(8,128)} %master_ref.1, f32[64,640]{1,0:T(8,128)} %m_ref.1, f32[64,640]{1,0:T(8,128)} %v_ref.1), custom_call_target="tpu_custom_call" | custom-call | tf_op jit(solution)/shard_map/left_factor/pallas_call | solution.py:108
  14.4 0.0 copy-start
  14.4 0.0 copy-start.1
  14.4 0.0 copy-start.2
  14.4 0.0 all-gather.3.cloned.1.call-update
  14.4 22.4 %all_to_all.20 = bf16[128,8,128]{2,1,0:T(8,128)(2,1)S(1)} all-to-all(bf16[128,8,128]{2,1,0:T(8,128)(2,1)S(1)} %bitcast.11), channel_id=1, replica_groups=mesh['dp'=32,'mp'=4] {'dp','mp'}, dimensions={0} | all-to-all | bytes 524288 | tf_op jit(solution)/shard_map/all_to_all | solution.py:404
  36.9 0.2 sum_repeat.1
  37.0 17.9 %all_to_all.21 = f32[128,8,128]{2,1,0:T(8,128)S(1)} all-to-all(f32[128,8,128]{2,1,0:T(8,128)S(1)} %sum_repeat.1), channel_id=1, replica_groups=mesh['dp'=32,'mp'=4] {'dp','mp'}, dimensions={0} | all-to-all | bytes 1048576 | tf_op jit(solution)/shard_map/all_to_all | solution.py:406
  55.0 5.1 %right_factor.1 = (bf16[2048,128]{1,0:T(8,128)(2,1)S(1)}, f32[64,128]{1,0:T(8,128)S(1)}, bf16[64,640]{1,0:T(8,128)(2,1)S(1)}) custom-call(f32[1024,128]{1,0:T(8,128)S(1)} %bitcast.9, f32[2,1024,640]{2,1,0:T(8,128)} %get-tuple-element.19.merged_hbm), custom_call_target="tpu_custom_call" | custom-call | tf_op jit(solution)/shard_map/right_factor/pallas_call | solution.py:247
  60.1 11.3 %all_to_all.22 = bf16[32,2,640]{2,1,0:T(2,128)(2,1)S(1)} all-to-all(bf16[32,2,640]{2,1,0:T(2,128)(2,1)S(1)} %reshape.39), channel_id=1, replica_groups=mesh['dp'=32,'mp'=4] {'dp'}, dimensions={0} | all-to-all | bytes 163840 | tf_op jit(solution)/shard_map/all_to_all | solution.py:408
  71.4 0.1 reduce_sum.12
  71.5 0.2 broadcast_in_dim.4
  71.7 16.1 %all_to_all.23 = bf16[128,2,640]{2,1,0:T(2,128)(2,1)S(1)} all-to-all(bf16[128,2,640]{2,1,0:T(2,128)(2,1)S(1)} %broadcast_in_dim.4), channel_id=1, replica_groups=mesh['dp'=32,'mp'=4] {'mp','dp'}, dimensions={0} | all-to-all | bytes 655360 | tf_op jit(solution)/shard_map/all_to_all | solution.py:411
  87.8 0.1 reshape.40.q_ref
  87.9 0.0 all-gather.3.cloned.1.call-done
  88.0 0.0 copy-done
  88.0 0.0 copy-done.1
  88.0 0.0 copy-done.2
  88.0 8.6 %decode_update.1 = (f32[2048,640]{1,0:T(8,128)}, bf16[2048,640]{1,0:T(8,128)(2,1)}, f32[64,640]{1,0:T(8,128)}, f32[64,640]{1,0:T(8,128)}, f32[64,640]{1,0:T(8,128)}, /*index=5*/f32[64,640]{1,0:T(8,128)}) custom-call(bf16[4,64,640]{2,1,0:T(8,128)(2,1)S(1)} %reshape.40.q_ref, bf16[2048,128]{1,0:T(8,128)(2,1)S(1)} %get-tuple-element.21.orth_ref, ...), custom_call_target="tpu_custom_call" | custom-call | tf_op jit(solution)/shard_map/decode_update/pallas_call | solution.py:368
  (1 shorter events, 0.0 us)
Async XLA Ops:
  7.2 80.8 %all-gather.3.cloned.1.call-start = ((), (), s32[]{:S(2)}) async-start(), calls=%async_computation.4 | async-start | bytes 8110080 | tf_op jit(solution)/shard_map/all_gather | solution.py:403
  14.4 73.6 %copy-start = (f32[64,640]{1,0:T(8,128)S(1)}, f32[64,640]{1,0:T(8,128)}, u32[]{:S(2)}) copy-start(f32[64,640]{1,0:T(8,128)} %master_ref.1) | copy-start | bytes 491524
  14.4 73.6 %copy-start.1 = (f32[64,640]{1,0:T(8,128)S(1)}, f32[64,640]{1,0:T(8,128)}, u32[]{:S(2)}) copy-start(f32[64,640]{1,0:T(8,128)} %m_ref.1) | copy-start | bytes 491524
  14.4 73.6 %copy-start.2 = (f32[64,640]{1,0:T(8,128)S(1)}, f32[64,640]{1,0:T(8,128)}, u32[]{:S(2)}) copy-start(f32[64,640]{1,0:T(8,128)} %v_ref.1) | copy-start | bytes 491524
Sparse Core Ops, SparseCore 0:
  14.6 56.3 all-gather.2

commit v5 on v4

--- a/solution.py
+++ b/solution.py
@@ -3,13 +3,14 @@
 from jax import lax
 from jax.experimental import pallas as pl
 from jax.experimental.pallas import tpu as pltpu
-from jax.sharding import PartitionSpec as P
+from jax.sharding import Mesh, PartitionSpec as P
 
 D = 2048
 HID = 2560
 STEP = 100
 RANK = 64
 REPLICAS = 32
+DP = ("y", "x", "c")
 HALF = D // 2
 COLS = 640
 ROWS = 64
@@ -137,14 +138,14 @@
 
 
 def sum_kernel(parts_ref, out_ref):
-    total = jnp.sum(parts_ref[...].astype(f32).reshape(out_ref.shape), axis=0, keepdims=True)
+    total = jnp.sum(parts_ref[...].astype(f32).reshape(128, 8, 128), axis=0, keepdims=True)
     out_ref[...] = jnp.broadcast_to(total, out_ref.shape)
 
 
 def sum_repeat(parts):
     return pl.pallas_call(
         sum_kernel,
-        out_shape=jax.ShapeDtypeStruct((128, 8, 128), f32),
+        out_shape=jax.ShapeDtypeStruct((64, 8, 128), f32),
         in_specs=[pl.BlockSpec(memory_space=pltpu.VMEM)],
         out_specs=pl.BlockSpec(memory_space=pltpu.VMEM),
         compiler_params=pltpu.CompilerParams(vmem_limit_bytes=16 * MIB),
@@ -201,7 +202,7 @@
     return square + pltpu.roll(square, RANK, 1)
 
 
-def right_kernel(p_ref, merged_hbm, orth_ref, square_ref, part_ref, merged_ref, sems):
+def right_kernel(own_ref, other_ref, merged_hbm, orth_ref, square_ref, part_ref, merged_ref, sems):
     def copy(c):
         half, rows = c // 4, pl.ds(c % 4 * BLOCK, BLOCK)
         return pltpu.make_async_copy(
@@ -210,7 +211,10 @@
 
     for c in range(RIGHT_AHEAD):
         copy(c).start()
-    pairs = pair_rows(p_ref[...])
+    own, other = own_ref[...], other_ref[...]
+    first = lax.axis_index("c") == 0
+    packed = jnp.concatenate([jnp.where(first, own, other), jnp.where(first, other, own)], axis=0)
+    pairs = pair_rows(packed)
     acc = [jnp.zeros((2 * RANK, COLS), f32)]
 
     def multiply(c):
@@ -243,7 +247,7 @@
     square_ref[...] = pair_gram(halves)
 
 
-def right(packed, merged):
+def right(own, other, merged):
     return pl.pallas_call(
         right_kernel,
         out_shape=(
@@ -252,6 +256,7 @@
             jax.ShapeDtypeStruct((RANK, COLS), bf16),
         ),
         in_specs=[
+            pl.BlockSpec(memory_space=pltpu.VMEM),
             pl.BlockSpec(memory_space=pltpu.VMEM),
             pl.BlockSpec(memory_space=pltpu.HBM),
         ],
@@ -262,7 +267,7 @@
         ],
         compiler_params=pltpu.CompilerParams(vmem_limit_bytes=16 * MIB),
         name="right_factor",
-    )(packed, hbm(merged))
+    )(own, other, hbm(merged))
 
 
 def adam(update, master, m_state, v_state):
@@ -321,11 +326,11 @@
         gram = gram + dot(q_ref[z], q_ref[z], 1, 1)
     total = jnp.sum(gram * square_ref[:, :RANK], keepdims=True)
     scale = 1.0 / jnp.sqrt(total / (D * HID) + norm_eps)
-    q = q_ref[lax.axis_index("mp")]
+    q = q_ref[lax.axis_index("z")]
     both_ref[:RANK] = q
     both_ref[RANK:] = q
     q_out[...] = q.astype(f32)
-    start = pl.multiple_of(lax.axis_index("dp") * ROWS, ROWS)
+    start = pl.multiple_of(lax.axis_index(DP) * ROWS, ROWS)
     decoded = dot(orth_ref[pl.ds(start, ROWS)], both_ref[...], 1, 0)
     owned = adam(decoded * scale, master_ref[...], m_ref[...], v_ref[...])
     small = [pltpu.make_async_copy(q_out, q_hbm, small_sems.at[3])]
@@ -400,15 +405,16 @@
 
 def shards(grads, errors, q_init, master, m_state, v_state):
     merged, part, states = left(grads, errors, q_init, master, m_state, v_state)
-    states = lax.all_gather(states, "dp", axis=0, tiled=False)
-    parts = lax.all_to_all(part.reshape(128, 8, 128), ("dp", "mp"), 0, 0)
+    states = lax.all_gather(states, DP, axis=0, tiled=False)
+    parts = lax.all_to_all(part.reshape(128, 8, 128), ("c", "y", "x", "z"), 0, 0)
     owned = sum_repeat(parts.reshape(HALF, 128))
-    packed = lax.all_to_all(owned, ("dp", "mp"), 0, 0).reshape(HALF, 128)
-    orth, square, q_part = right(packed, merged)
-    q_parts = lax.all_to_all(q_part.reshape(32, 2, COLS), "dp", 0, 0)
+    own = lax.all_to_all(owned, ("y", "x", "z"), 0, 0).reshape(HALF // 2, 128)
+    other = lax.ppermute(own, "c", [(0, 1), (1, 0)])
+    orth, square, q_part = right(own, other, merged)
+    q_parts = lax.all_to_all(q_part.reshape(32, 2, COLS), DP, 0, 0)
     q_owned = jnp.sum(q_parts.astype(f32), axis=0).astype(bf16)
     q_owned = jnp.broadcast_to(q_owned[None], (128, 2, COLS))
-    q_all = lax.all_to_all(q_owned, ("mp", "dp"), 0, 0).reshape(4, RANK, COLS)
+    q_all = lax.all_to_all(q_owned, ("z",) + DP, 0, 0).reshape(4, RANK, COLS)
     error_new, weights, q_new, master_new, m_new, v_new = final(
         q_all, orth, square, merged, states, master, m_state, v_state
     )
@@ -416,20 +422,22 @@
 
 
 def solution(mesh):
+    replicas, columns = mesh.devices.shape
+    mesh = Mesh(mesh.devices.reshape(4, replicas // 8, 2, columns), DP + ("z",))
     in_specs = (
-        P("dp", None, "mp"),
-        P("dp", None, "mp"),
-        P("mp", None),
-        P("dp", "mp"),
-        P("dp", "mp"),
-        P("dp", "mp"),
+        P(DP, None, "z"),
+        P(DP, None, "z"),
+        P("z", None),
+        P(DP, "z"),
+        P(DP, "z"),
+        P(DP, "z"),
     )
     out_specs = (
-        P("dp", None, "mp"),
-        P("mp", None),
-        P("dp", "mp"),
-        P("dp", "mp"),
-        P("dp", "mp"),
-        P(None, "mp"),
+        P(DP, None, "z"),
+        P("z", None),
+        P(DP, "z"),
+        P(DP, "z"),
+        P(DP, "z"),
+        P(None, "z"),
     )
     return jax.shard_map(shards, mesh=mesh, in_specs=in_specs, out_specs=out_specs, check_vma=False)

time: 104 us -> 103 us (level)
  blocking collectives: 67.8 us -> 63.8 us
  starting transfers between devices: 0.04 us -> 2.12 us
  waiting for transfers between devices: 0.04 us -> 1.2 us
    all_to_all x4, blocking collectives: 67.8 us -> 63.8 us  [the longest x1 21.9 us: shards(): lax.all_to_all(part.reshape(128, 8, 128), ('c', 'y', 'x', 'z'), 0, 0)]
    ppermute x0 -> x1, starting transfers between devices: none -> 2.09 us  [shards(): other = lax.ppermute(own, 'c', [(0, 1), (1, 0)])]
    ppermute x0 -> x1, waiting for transfers between devices: none -> 1.16 us  [shards(): other = lax.ppermute(own, 'c', [(0, 1), (1, 0)])]
  transfers between devices with their start and end apart: 1 -> 2, of which waited for: 0 -> 1; matrix products, arithmetic and copies ran while one was open for 0% -> 0% of each run, Pallas kernels for 5% -> 5%
where the time goes in v5:
time: 103 us
  blocking collectives  63.8 us (62%)
  Pallas kernels  21 us (20%)
  between operations  14.1 us (14%)
  starting transfers between devices  2.12 us (2%)
  waiting for transfers between devices  1.2 us (1%)
    all_to_all x1, blocking collectives, shards(): lax.all_to_all(part.reshape(128, 8, 128), ('c', 'y', 'x', 'z'), 0, 0)  21.9 us
    all_to_all x1, blocking collectives, shards(): q_all = lax.all_to_all(q_owned, ('z',) + DP, 0, 0).reshape(4, RANK, COLS)  15.4 us
    all_to_all x1, blocking collectives, shards(): own = lax.all_to_all(owned, ('y', 'x', 'z'), 0, 0).reshape(HALF // 2, 128)  14.7 us
    all_to_all x1, blocking collectives, shards(): q_parts = lax.all_to_all(q_part.reshape(32, 2, COLS), DP, 0, 0)  11.8 us
    pallas_call x1, Pallas kernels, final(): pl.pallas_call(final_kernel, out_shape=(jax.ShapeDtypeStruct((D, COLS), f...  8.6 us
    pallas_call x1, Pallas kernels, left(): pl.pallas_call(left_kernel, out_shape=(pltpu.HBM((2, HALF, COLS), f32), j...  7.16 us
    pallas_call x1, Pallas kernels, right(): pl.pallas_call(right_kernel, out_shape=(jax.ShapeDtypeStruct((D, 2 * RANK...  5.11 us
    ppermute x1, starting transfers between devices, shards(): other = lax.ppermute(own, 'c', [(0, 1), (1, 0)])  2.09 us
  transfers between devices with their start and end apart: 2, of which 1 were waited for; matrix products, arithmetic and copies ran while one was open for 0% of the time, Pallas kernels for 5%

profile of v5, /device:TPU:1, one launch (start us, length us, event | category | flops | bytes accessed | tf_op | source)
XLA Modules:
  0.0 102.7 jit_solution(3067162100356532619)
XLA Ops:
  7.2 0.0 all-gather.3.cloned.1.call-start
  7.2 7.2 %left_factor.1 = (f32[2,1024,640]{2,1,0:T(8,128)}, bf16[1024,128]{1,0:T(8,128)(2,1)S(1)}, bf16[3,64,640]{2,1,0:T(8,128)(2,1)}) custom-call(f32[2,1024,640]{2,1,0:T(8,128)} %bitcast.14, f32[2,1024,640]{2,1,0:T(8,128)} %bitcast.15, f32[64,640]{1,0:T(8,128)} %bitcast.16, f32[64,640]{1,0:T(8,128)} %master_ref.1, f32[64,640]{1,0:T(8,128)} %m_ref.1, f32[64,640]{1,0:T(8,128)} %v_ref.1), custom_call_target="tpu_custom_call" | custom-call | tf_op jit(solution)/shard_map/left_factor/pallas_call | solution.py:109
  14.4 0.0 copy-start
  14.4 0.0 copy-start.1
  14.4 0.0 copy-start.2
  14.4 0.0 all-gather.3.cloned.1.call-update
  14.4 21.9 %all_to_all.20 = bf16[128,8,128]{2,1,0:T(8,128)(2,1)S(1)} all-to-all(bf16[128,8,128]{2,1,0:T(8,128)(2,1)S(1)} %bitcast.12), channel_id=1, replica_groups=mesh['y'=4,'x'=4,'c'=2,'z'=4] {'c','y','x','z'}, dimensions={0} | all-to-all | bytes 524288 | tf_op jit(solution)/shard_map/all_to_all | solution.py:409
  36.4 0.2 sum_repeat.1
  36.5 14.7 %all_to_all.21 = f32[64,8,128]{2,1,0:T(8,128)S(1)} all-to-all(f32[64,8,128]{2,1,0:T(8,128)S(1)} %sum_repeat.1), channel_id=1, replica_groups=mesh['y'=4,'x'=4,'c'=2,'z'=4] {'y','x','z'}, dimensions={0} | all-to-all | bytes 524288 | tf_op jit(solution)/shard_map/all_to_all | solution.py:411
  51.2 2.1 %collective-permute-start = (f32[512,128]{1,0:T(8,128)S(1)}, f32[512,128]{1,0:T(8,128)S(1)}, u32[]{:S(2)}, u32[]{:S(2)}) collective-permute-start(f32[512,128]{1,0:T(8,128)S(1)} %bitcast.9), channel_id=1, source_target_pairs={{0,4},{4,0},{1,5},{5,1},{2,6},{6,2},{3,7},{7,3},{8,12},{12,8},{9,1... | collective-permute-start | bytes 786440 | tf_op jit(solution)/shard_map/ppermute | solution.py:412
  53.3 1.2 %collective-permute-done.other_ref = f32[512,128]{1,0:T(8,128)S(1)} collective-permute-done((f32[512,128]{1,0:T(8,128)S(1)}, f32[512,128]{1,0:T(8,128)S(1)}, u32[]{:S(2)}, u32[]{:S(2)}) %collective-permute-start) | collective-permute-done | bytes 262176 | tf_op jit(solution)/shard_map/ppermute | solution.py:412
  54.4 5.1 %right_factor.1 = (bf16[2048,128]{1,0:T(8,128)(2,1)S(1)}, f32[64,128]{1,0:T(8,128)S(1)}, bf16[64,640]{1,0:T(8,128)(2,1)S(1)}) custom-call(f32[512,128]{1,0:T(8,128)S(1)} %bitcast.10, f32[512,128]{1,0:T(8,128)S(1)} %collective-permute-done.other_ref, f32[2,1024,640]{2,1,0:T(8,128)} %get-tuple-element.19.merged_hbm), custom_call_target="tpu_custom_call" | custom-call | tf_op jit(solution)/shard_map/right_factor/pallas_call | solution.py:251
  59.6 11.8 %all_to_all.22 = bf16[32,2,640]{2,1,0:T(2,128)(2,1)S(1)} all-to-all(bf16[32,2,640]{2,1,0:T(2,128)(2,1)S(1)} %reshape.39), channel_id=1, replica_groups=mesh['y'=4,'x'=4,'c'=2,'z'=4] {'y','x','c'}, dimensions={0} | all-to-all | bytes 163840 | tf_op jit(solution)/shard_map/all_to_all | solution.py:414
  71.4 0.1 reduce_sum.12
  71.5 0.2 broadcast_in_dim.4
  71.7 15.4 %all_to_all.23 = bf16[128,2,640]{2,1,0:T(2,128)(2,1)S(1)} all-to-all(bf16[128,2,640]{2,1,0:T(2,128)(2,1)S(1)} %broadcast_in_dim.4), channel_id=1, replica_groups=mesh['y'=4,'x'=4,'c'=2,'z'=4] {'z','y','x','c'}, dimensions={0} | all-to-all | bytes 655360 | tf_op jit(solution)/shard_map/all_to_all | solution.py:417
  87.1 0.1 reshape.40.q_ref
  87.2 0.0 all-gather.3.cloned.1.call-done
  87.2 0.0 copy-done
  87.2 0.0 copy-done.1
  87.2 0.0 copy-done.2
  87.2 8.6 %decode_update.1 = (f32[2048,640]{1,0:T(8,128)}, bf16[2048,640]{1,0:T(8,128)(2,1)}, f32[64,640]{1,0:T(8,128)}, f32[64,640]{1,0:T(8,128)}, f32[64,640]{1,0:T(8,128)}, /*index=5*/f32[64,640]{1,0:T(8,128)}) custom-call(bf16[4,64,640]{2,1,0:T(8,128)(2,1)S(1)} %reshape.40.q_ref, bf16[2048,128]{1,0:T(8,128)(2,1)S(1)} %get-tuple-element.21.orth_ref, ...), custom_call_target="tpu_custom_call" | custom-call | tf_op jit(solution)/shard_map/decode_update/pallas_call | solution.py:373
  (1 shorter events, 0.0 us)
Async XLA Ops:
  7.2 80.0 %all-gather.3.cloned.1.call-start = ((), (), s32[]{:S(2)}) async-start(), calls=%async_computation.4 | async-start | bytes 8110080 | tf_op jit(solution)/shard_map/all_gather | solution.py:408
  14.4 72.8 %copy-start = (f32[64,640]{1,0:T(8,128)S(1)}, f32[64,640]{1,0:T(8,128)}, u32[]{:S(2)}) copy-start(f32[64,640]{1,0:T(8,128)} %master_ref.1) | copy-start | bytes 491524
  14.4 72.8 %copy-start.1 = (f32[64,640]{1,0:T(8,128)S(1)}, f32[64,640]{1,0:T(8,128)}, u32[]{:S(2)}) copy-start(f32[64,640]{1,0:T(8,128)} %m_ref.1) | copy-start | bytes 491524
  14.4 72.8 %copy-start.2 = (f32[64,640]{1,0:T(8,128)S(1)}, f32[64,640]{1,0:T(8,128)}, u32[]{:S(2)}) copy-start(f32[64,640]{1,0:T(8,128)} %v_ref.1) | copy-start | bytes 491524
  51.2 3.2 %collective-permute-start = (f32[512,128]{1,0:T(8,128)S(1)}, f32[512,128]{1,0:T(8,128)S(1)}, u32[]{:S(2)}, u32[]{:S(2)}) collective-permute-start(f32[512,128]{1,0:T(8,128)S(1)} %bitcast.9), channel_id=1, source_target_pairs={{0,4},{4,0},{1,5},{5,1},{2,6},{6,2},{3,7},{7,3},{8,12},{12,8},{9,1... | collective-permute-start | bytes 786440 | tf_op jit(solution)/shard_map/ppermute | solution.py:412
Sparse Core Ops, SparseCore 0:
  14.6 56.5 all-gather.2

commit v6 on v5

--- a/solution.py
+++ b/solution.py
@@ -29,7 +29,7 @@
 LEFT_CHUNKS = 8
 AHEAD = 5
 DELAY = 2
-RIGHT_AHEAD = 3
+RIGHT_AHEAD = 4
 BLOCK = 256
 
 

time: 103 us -> 102 us (level)
  no operation moved by 1% of the time
where the time goes in v6:
time: 102 us
  blocking collectives  63.4 us (62%)
  Pallas kernels  20.8 us (20%)
  between operations  14.1 us (14%)
  starting transfers between devices  2.12 us (2%)
  waiting for transfers between devices  1.2 us (1%)
    all_to_all x1, blocking collectives, shards(): lax.all_to_all(part.reshape(128, 8, 128), ('c', 'y', 'x', 'z'), 0, 0)  21.9 us
    all_to_all x1, blocking collectives, shards(): q_all = lax.all_to_all(q_owned, ('z',) + DP, 0, 0).reshape(4, RANK, COLS)  15 us
    all_to_all x1, blocking collectives, shards(): own = lax.all_to_all(owned, ('y', 'x', 'z'), 0, 0).reshape(HALF // 2, 128)  14.7 us
    all_to_all x1, blocking collectives, shards(): q_parts = lax.all_to_all(q_part.reshape(32, 2, COLS), DP, 0, 0)  11.8 us
    pallas_call x1, Pallas kernels, final(): pl.pallas_call(final_kernel, out_shape=(jax.ShapeDtypeStruct((D, COLS), f...  8.61 us
    pallas_call x1, Pallas kernels, left(): pl.pallas_call(left_kernel, out_shape=(pltpu.HBM((2, HALF, COLS), f32), j...  7.16 us
    pallas_call x1, Pallas kernels, right(): pl.pallas_call(right_kernel, out_shape=(jax.ShapeDtypeStruct((D, 2 * RANK...  4.93 us
    ppermute x1, starting transfers between devices, shards(): other = lax.ppermute(own, 'c', [(0, 1), (1, 0)])  2.09 us
  transfers between devices with their start and end apart: 2, of which 1 were waited for; matrix products, arithmetic and copies ran while one was open for 0% of the time, Pallas kernels for 5%

profile of v6, /device:TPU:1, one launch (start us, length us, event | category | flops | bytes accessed | tf_op | source)
XLA Modules:
  0.0 102.2 jit_solution(9371549489862531145)
XLA Ops:
  7.2 0.0 all-gather.3.cloned.1.call-start
  7.2 7.2 %left_factor.1 = (f32[2,1024,640]{2,1,0:T(8,128)}, bf16[1024,128]{1,0:T(8,128)(2,1)S(1)}, bf16[3,64,640]{2,1,0:T(8,128)(2,1)}) custom-call(f32[2,1024,640]{2,1,0:T(8,128)} %bitcast.14, f32[2,1024,640]{2,1,0:T(8,128)} %bitcast.15, f32[64,640]{1,0:T(8,128)} %bitcast.16, f32[64,640]{1,0:T(8,128)} %master_ref.1, f32[64,640]{1,0:T(8,128)} %m_ref.1, f32[64,640]{1,0:T(8,128)} %v_ref.1), custom_call_target="tpu_custom_call" | custom-call | tf_op jit(solution)/shard_map/left_factor/pallas_call | solution.py:109
  14.4 0.0 copy-start
  14.4 0.0 copy-start.1
  14.4 0.0 copy-start.2
  14.4 0.0 all-gather.3.cloned.1.call-update
  14.4 21.9 %all_to_all.20 = bf16[128,8,128]{2,1,0:T(8,128)(2,1)S(1)} all-to-all(bf16[128,8,128]{2,1,0:T(8,128)(2,1)S(1)} %bitcast.12), channel_id=1, replica_groups=mesh['y'=4,'x'=4,'c'=2,'z'=4] {'c','y','x','z'}, dimensions={0} | all-to-all | bytes 524288 | tf_op jit(solution)/shard_map/all_to_all | solution.py:409
  36.4 0.2 sum_repeat.1
  36.5 14.7 %all_to_all.21 = f32[64,8,128]{2,1,0:T(8,128)S(1)} all-to-all(f32[64,8,128]{2,1,0:T(8,128)S(1)} %sum_repeat.1), channel_id=1, replica_groups=mesh['y'=4,'x'=4,'c'=2,'z'=4] {'y','x','z'}, dimensions={0} | all-to-all | bytes 524288 | tf_op jit(solution)/shard_map/all_to_all | solution.py:411
  51.2 2.1 %collective-permute-start = (f32[512,128]{1,0:T(8,128)S(1)}, f32[512,128]{1,0:T(8,128)S(1)}, u32[]{:S(2)}, u32[]{:S(2)}) collective-permute-start(f32[512,128]{1,0:T(8,128)S(1)} %bitcast.9), channel_id=1, source_target_pairs={{0,4},{4,0},{1,5},{5,1},{2,6},{6,2},{3,7},{7,3},{8,12},{12,8},{9,1... | collective-permute-start | bytes 786440 | tf_op jit(solution)/shard_map/ppermute | solution.py:412
  53.3 1.2 %collective-permute-done.other_ref = f32[512,128]{1,0:T(8,128)S(1)} collective-permute-done((f32[512,128]{1,0:T(8,128)S(1)}, f32[512,128]{1,0:T(8,128)S(1)}, u32[]{:S(2)}, u32[]{:S(2)}) %collective-permute-start) | collective-permute-done | bytes 262176 | tf_op jit(solution)/shard_map/ppermute | solution.py:412
  54.4 4.9 %right_factor.1 = (bf16[2048,128]{1,0:T(8,128)(2,1)S(1)}, f32[64,128]{1,0:T(8,128)S(1)}, bf16[64,640]{1,0:T(8,128)(2,1)S(1)}) custom-call(f32[512,128]{1,0:T(8,128)S(1)} %bitcast.10, f32[512,128]{1,0:T(8,128)S(1)} %collective-permute-done.other_ref, f32[2,1024,640]{2,1,0:T(8,128)} %get-tuple-element.19.merged_hbm), custom_call_target="tpu_custom_call" | custom-call | tf_op jit(solution)/shard_map/right_factor/pallas_call | solution.py:251
  59.4 11.8 %all_to_all.22 = bf16[32,2,640]{2,1,0:T(2,128)(2,1)S(1)} all-to-all(bf16[32,2,640]{2,1,0:T(2,128)(2,1)S(1)} %reshape.39), channel_id=1, replica_groups=mesh['y'=4,'x'=4,'c'=2,'z'=4] {'y','x','c'}, dimensions={0} | all-to-all | bytes 163840 | tf_op jit(solution)/shard_map/all_to_all | solution.py:414
  71.3 0.1 reduce_sum.12
  71.3 0.2 broadcast_in_dim.4
  71.5 15.0 %all_to_all.23 = bf16[128,2,640]{2,1,0:T(2,128)(2,1)S(1)} all-to-all(bf16[128,2,640]{2,1,0:T(2,128)(2,1)S(1)} %broadcast_in_dim.4), channel_id=1, replica_groups=mesh['y'=4,'x'=4,'c'=2,'z'=4] {'z','y','x','c'}, dimensions={0} | all-to-all | bytes 655360 | tf_op jit(solution)/shard_map/all_to_all | solution.py:417
  86.5 0.1 reshape.40.q_ref
  86.6 0.0 all-gather.3.cloned.1.call-done
  86.7 0.0 copy-done
  86.7 0.0 copy-done.1
  86.7 0.0 copy-done.2
  86.7 8.6 %decode_update.1 = (f32[2048,640]{1,0:T(8,128)}, bf16[2048,640]{1,0:T(8,128)(2,1)}, f32[64,640]{1,0:T(8,128)}, f32[64,640]{1,0:T(8,128)}, f32[64,640]{1,0:T(8,128)}, /*index=5*/f32[64,640]{1,0:T(8,128)}) custom-call(bf16[4,64,640]{2,1,0:T(8,128)(2,1)S(1)} %reshape.40.q_ref, bf16[2048,128]{1,0:T(8,128)(2,1)S(1)} %get-tuple-element.21.orth_ref, ...), custom_call_target="tpu_custom_call" | custom-call | tf_op jit(solution)/shard_map/decode_update/pallas_call | solution.py:373
  (1 shorter events, 0.0 us)
Async XLA Ops:
  7.2 79.5 %all-gather.3.cloned.1.call-start = ((), (), s32[]{:S(2)}) async-start(), calls=%async_computation.4 | async-start | bytes 8110080 | tf_op jit(solution)/shard_map/all_gather | solution.py:408
  14.4 72.3 %copy-start = (f32[64,640]{1,0:T(8,128)S(1)}, f32[64,640]{1,0:T(8,128)}, u32[]{:S(2)}) copy-start(f32[64,640]{1,0:T(8,128)} %master_ref.1) | copy-start | bytes 491524
  14.4 72.3 %copy-start.1 = (f32[64,640]{1,0:T(8,128)S(1)}, f32[64,640]{1,0:T(8,128)}, u32[]{:S(2)}) copy-start(f32[64,640]{1,0:T(8,128)} %m_ref.1) | copy-start | bytes 491524
  14.4 72.3 %copy-start.2 = (f32[64,640]{1,0:T(8,128)S(1)}, f32[64,640]{1,0:T(8,128)}, u32[]{:S(2)}) copy-start(f32[64,640]{1,0:T(8,128)} %v_ref.1) | copy-start | bytes 491524
  51.2 3.2 %collective-permute-start = (f32[512,128]{1,0:T(8,128)S(1)}, f32[512,128]{1,0:T(8,128)S(1)}, u32[]{:S(2)}, u32[]{:S(2)}) collective-permute-start(f32[512,128]{1,0:T(8,128)S(1)} %bitcast.9), channel_id=1, source_target_pairs={{0,4},{4,0},{1,5},{5,1},{2,6},{6,2},{3,7},{7,3},{8,12},{12,8},{9,1... | collective-permute-start | bytes 786440 | tf_op jit(solution)/shard_map/ppermute | solution.py:412
Sparse Core Ops, SparseCore 0:
  14.6 56.5 all-gather.2
